TPU v7x, 32 devices: a whole 2x2x4 slice. The times are simulated.
32 devices in a mesh: seq: 8 (over y, x, core), head: 4 (over z).
Axes of the slice: x: 2, y: 2, z: 4, core: 2. Of those that a mesh axis runs over, the one named last changes fastest.
Arguments:
- queries: bfloat16 [2048, 4096], P(('seq', 'head')), may hold values from -72 to 72
- keys: bfloat16 [2048, 2048], P(('seq', 'head')), may hold values from -6 to 6
- values: bfloat16 [2048, 2048], P(('seq', 'head')), may hold values from -6 to 6
- prefix_keys: bfloat16 [4096, 2048], P(None, 'head'), may hold values from -10 to 10
- prefix_values: bfloat16 [4096, 2048], P(None, 'head'), may hold values from -6 to 6
- span_start: int32 [1], replicated, may hold values from 0 to 4095
Outputs:
- attended: bfloat16 [2048, 4096], P(('seq', 'head'))
All inputs are finite; a program needn't handle non-finite values.
Results may differ from a plain program's by a relative error of at most 0.003.
Values may be sent and summed in bfloat16 or wider, within the bound.
No kernel may reach another device: no remote copies, remote signals or barrier semaphores. Data moves between devices by JAX's collectives and lax.ppermute only.
A program may use at most 128 MiB of HBM per device.

v0:
```python
import jax
import jax.numpy as jnp
from jax import lax
from jax.sharding import PartitionSpec as P

HEAD_DIM = 128
QH = 32
KVH = 16
QSCALE = 144
WINDOW = 4096


def shifted(shard, axis, by):
    size = lax.axis_size(axis)
    pairs = [(i, i + by) for i in range(size) if 0 <= i + by < size]
    return lax.ppermute(shard, axis, pairs)


def shortened(shard):
    return jax.tree.map(lambda a: a.astype(jnp.bfloat16) if a.dtype == jnp.float32 else a, shard)


def attend_block(query_rows, key_rows, value_rows, query_first, key_first, start_value):
    block_rows = query_rows.shape[0]
    key_count = key_rows.shape[0]
    grouping = QH // KVH
    scaling = QSCALE ** (-0.5)
    local_groups = key_rows.shape[1] // HEAD_DIM
    query_pos = query_first + jnp.arange(block_rows, dtype=jnp.int32)
    key_pos = key_first + jnp.arange(key_count, dtype=jnp.int32)
    distance = query_pos[:, None] - key_pos[None, :]
    allowed = (distance >= 0) & (distance < WINDOW) & (start_value + key_pos >= 0)[None, :]
    outputs = []
    for key_group in range(local_groups):
        lower = key_group * grouping * HEAD_DIM
        query_head = query_rows[:, lower : lower + grouping * HEAD_DIM].reshape(
            block_rows, grouping, HEAD_DIM
        )
        key_head = key_rows[:, key_group * HEAD_DIM : (key_group + 1) * HEAD_DIM]
        value_head = value_rows[:, key_group * HEAD_DIM : (key_group + 1) * HEAD_DIM]
        scores = (
            jnp.einsum("qgd,kd->gqk", query_head, key_head, preferred_element_type=jnp.float32)
            * scaling
        )
        scores = jnp.where(allowed[None], scores, -jnp.inf)
        peak_score = jnp.max(scores, axis=2, keepdims=True)
        unnormed = jnp.exp(scores - peak_score)
        totals = jnp.sum(unnormed, axis=2)
        weights = unnormed.astype(jnp.bfloat16)
        mixture = jnp.einsum("gqk,kd->qgd", weights, value_head, preferred_element_type=jnp.float32)
        outputs.append(
            (mixture / jnp.transpose(totals)[:, :, None]).reshape(block_rows, grouping * HEAD_DIM)
        )
    return jnp.concatenate(outputs, axis=1).astype(jnp.bfloat16)


def shards(queries, keys, values, prefix_keys, prefix_values, span_start):
    query_local, key_local, value_local = (
        lax.all_to_all(queries, "head", split_axis=1, concat_axis=0, tiled=True),
        lax.all_to_all(keys, "head", split_axis=1, concat_axis=0, tiled=True),
        lax.all_to_all(values, "head", split_axis=1, concat_axis=0, tiled=True),
    )
    seq_rows = query_local.shape[0]
    shards_back = WINDOW // seq_rows
    seq_index = lax.axis_index("seq")

    def relay(step, carried):
        moving_keys, moving_values, window_keys, window_values = carried
        moving_keys, moving_values = shifted((moving_keys, moving_values), "seq", 1)
        offset = (shards_back - 1 - step) * seq_rows
        window_keys = lax.dynamic_update_slice_in_dim(window_keys, moving_keys, offset, 0)
        window_values = lax.dynamic_update_slice_in_dim(window_values, moving_values, offset, 0)
        return (moving_keys, moving_values, window_keys, window_values)

    empty = jnp.zeros((WINDOW, key_local.shape[1]), jnp.bfloat16)
    carried = lax.fori_loop(0, shards_back, relay, (key_local, value_local, empty, empty))
    window_keys = carried[2]
    window_values = carried[3]
    first_row = jnp.minimum(seq_index * seq_rows, WINDOW)
    padded_keys = jnp.concatenate([prefix_keys, jnp.zeros_like(prefix_keys)], axis=0)
    padded_values = jnp.concatenate([prefix_values, jnp.zeros_like(prefix_values)], axis=0)
    window_keys = window_keys + lax.dynamic_slice_in_dim(padded_keys, first_row, WINDOW, 0)
    window_values = window_values + lax.dynamic_slice_in_dim(padded_values, first_row, WINDOW, 0)
    all_keys = jnp.concatenate([window_keys, key_local], axis=0)
    all_values = jnp.concatenate([window_values, value_local], axis=0)
    block_rows = min(512, seq_rows)
    block_count = seq_rows // block_rows
    start_value = span_start[0]
    key_base = (seq_index - shards_back) * seq_rows
    query_base = seq_index * seq_rows

    def one_block(block_index):
        first = block_index * block_rows
        return attend_block(
            query_local, all_keys, all_values, query_base + first, key_base + first, start_value
        )

    blocks = lax.map(one_block, jnp.arange(block_count, dtype=jnp.int32))
    attended = blocks.reshape(seq_rows, query_local.shape[1])
    return lax.all_to_all(
        shortened(attended), "head", split_axis=0, concat_axis=1, tiled=True
    ).astype(attended.dtype)


def solution(mesh):
    placed = (
        P(("seq", "head"), None),
        P(("seq", "head"), None),
        P(("seq", "head"), None),
        P(None, "head"),
        P(None, "head"),
        P(),
    )
    return jax.shard_map(
        shards, mesh=mesh, in_specs=placed, out_specs=P(("seq", "head"), None), check_vma=False
    )
```

profile of v0, /device:TPU:1, one launch (start us, length us, event | category | flops | bytes accessed | tf_op | source)
XLA Modules:
  0.0 294.3 jit_solution(2028051749420258813)
XLA Ops:
  1.7 5.4 %all-to-all-start.1 = ((bf16[64,4,512]{2,0,1:T(8,128)(2,1)}), bf16[64,4,512]{2,0,1:T(8,128)(2,1)S(1)}, u32[]{:S(2)}, u32[]{:S(2)}) async-start(bf16[64,4,512]{2,0,1:T(8,128)(2,1)} %bitcast.99), calls=%async_computation.1 | async-start | bytes 524288 | tf_op jit(solution)/shard_map/all_to_all | solution.py:61
  9.4 5.2 %all-to-all-done.1 = bf16[64,4,512]{2,0,1:T(8,128)(2,1)S(1)} async-done(((bf16[64,4,512]{2,0,1:T(8,128)(2,1)}), bf16[64,4,512]{2,0,1:T(8,128)(2,1)S(1)}, u32[]{:S(2)}, u32[]{:S(2)}) %all-to-all-start.1) | async-done | bytes 262176 | tf_op jit(solution)/shard_map/all_to_all | solution.py:61
  14.7 3.4 %all-to-all-start = ((bf16[64,4,512]{2,0,1:T(8,128)(2,1)}), bf16[64,4,512]{2,0,1:T(8,128)(2,1)S(1)}, u32[]{:S(2)}, u32[]{:S(2)}) async-start(bf16[64,4,512]{2,0,1:T(8,128)(2,1)} %bitcast.100), calls=%async_computation | async-start | bytes 524288 | tf_op jit(solution)/shard_map/all_to_all | solution.py:60
  18.1 3.2 %fusion.21 = pred[256,4352]{0,1:T(8,128)(4,1)S(1)} fusion(s32[4352]{0:T(1024)S(1)} %iota_add_fusion, s32[256]{0:T(256)S(1)} %iota_add_fusion.1, pred[4352]{0:T(1024)(128)(4,1)S(1)} %add_compare_fusion), kind=kLoop, calls=%fused_computation.37 | loop fusion | flops 5570560 | bytes 1136896 | tf_op jit(solution)/shard_map/while/body/eval_jaxpr/and | solution.py:32
  23.2 6.4 %copy.62 = bf16[4096,512]{0,1:T(8,128)(2,1)} copy(bf16[4096,512]{1,0:T(8,128)(2,1)} %param.12) | data formatting | bytes 8388608 | tf_op args[4]
  29.7 4.5 %all-to-all-start.2 = ((bf16[64,4,1024]{2,0,1:T(8,128)(2,1)}), bf16[64,4,1024]{2,0,1:T(8,128)(2,1)S(1)}, u32[]{:S(2)}, u32[]{:S(2)}) async-start(bf16[64,4,1024]{2,0,1:T(8,128)(2,1)} %bitcast.98), calls=%async_computation.2 | async-start | bytes 1048576 | tf_op jit(solution)/shard_map/all_to_all | solution.py:59
  34.2 2.5 broadcast.92.clone
  38.9 192.1 %while.6 = (s32[]{:T(128)}, bf16[256,512]{1,0:T(8,128)(2,1)S(1)}, bf16[256,512]{1,0:T(8,128)(2,1)S(1)}, bf16[4096,512]{1,0:T(8,128)(2,1)}, bf16[4096,512]{0,1:T(...) while((s32[]{:T(128)}, bf16[256,512]{1,0:T(8,128)(2,1)S(1)}, ...), condition=%wide.region_1.0_spmd, body=%wide.region_0.0_spmd.sunk | while | flops 7 | bytes 4718839 | solution.py:76
  38.9 5.9 %collective-permute-start.1 = (bf16[256,512]{1,0:T(8,128)(2,1)S(1)}, bf16[256,512]{1,0:T(8,128)(2,1)S(1)}, u32[]{:S(2)}, u32[]{:S(2)}) collective-permute-start(bf16[256,512]{1,0:T(8,128)(2,1)S(1)} %get-tuple-element.196), channel_id=1, source_target_pairs={{0,4},{4,8},{8,12},{12,16},{16,20},{20,24},{24,28},{1,5},{5,9},{9,... | collective-permute-start | bytes 786440 | tf_op jit(solution)/shard_map/while/body/eval_jaxpr/ppermute | solution.py:16
  51.7 4.4 %collective-permute-start.1 = (bf16[256,512]{1,0:T(8,128)(2,1)S(1)}, bf16[256,512]{1,0:T(8,128)(2,1)S(1)}, u32[]{:S(2)}, u32[]{:S(2)}) collective-permute-start(bf16[256,512]{1,0:T(8,128)(2,1)S(1)} %get-tuple-element.196), channel_id=1, source_target_pairs={{0,4},{4,8},{8,12},{12,16},{16,20},{20,24},{24,28},{1,5},{5,9},{9,... | collective-permute-start | bytes 786440 | tf_op jit(solution)/shard_map/while/body/eval_jaxpr/ppermute | solution.py:16
  62.9 4.4 %collective-permute-start.1 = (bf16[256,512]{1,0:T(8,128)(2,1)S(1)}, bf16[256,512]{1,0:T(8,128)(2,1)S(1)}, u32[]{:S(2)}, u32[]{:S(2)}) collective-permute-start(bf16[256,512]{1,0:T(8,128)(2,1)S(1)} %get-tuple-element.196), channel_id=1, source_target_pairs={{0,4},{4,8},{8,12},{12,16},{16,20},{20,24},{24,28},{1,5},{5,9},{9,... | collective-permute-start | bytes 786440 | tf_op jit(solution)/shard_map/while/body/eval_jaxpr/ppermute | solution.py:16
  74.1 4.4 %collective-permute-start.1 = (bf16[256,512]{1,0:T(8,128)(2,1)S(1)}, bf16[256,512]{1,0:T(8,128)(2,1)S(1)}, u32[]{:S(2)}, u32[]{:S(2)}) collective-permute-start(bf16[256,512]{1,0:T(8,128)(2,1)S(1)} %get-tuple-element.196), channel_id=1, source_target_pairs={{0,4},{4,8},{8,12},{12,16},{16,20},{20,24},{24,28},{1,5},{5,9},{9,... | collective-permute-start | bytes 786440 | tf_op jit(solution)/shard_map/while/body/eval_jaxpr/ppermute | solution.py:16
  78.5 2.8 collective-permute-start
  85.4 4.4 %collective-permute-start.1 = (bf16[256,512]{1,0:T(8,128)(2,1)S(1)}, bf16[256,512]{1,0:T(8,128)(2,1)S(1)}, u32[]{:S(2)}, u32[]{:S(2)}) collective-permute-start(bf16[256,512]{1,0:T(8,128)(2,1)S(1)} %get-tuple-element.196), channel_id=1, source_target_pairs={{0,4},{4,8},{8,12},{12,16},{16,20},{20,24},{24,28},{1,5},{5,9},{9,... | collective-permute-start | bytes 786440 | tf_op jit(solution)/shard_map/while/body/eval_jaxpr/ppermute | solution.py:16
  89.8 3.7 %collective-permute-start = (bf16[256,512]{1,0:T(8,128)(2,1)S(1)}, bf16[256,512]{1,0:T(8,128)(2,1)S(1)}, u32[]{:S(2)}, u32[]{:S(2)}) collective-permute-start(bf16[256,512]{1,0:T(8,128)(2,1)S(1)} %get-tuple-element.195), channel_id=1, source_target_pairs={{0,4},{4,8},{8,12},{12,16},{16,20},{20,24},{24,28},{1,5},{5,9},{9,... | collective-permute-start | bytes 786440 | tf_op jit(solution)/shard_map/while/body/eval_jaxpr/ppermute | solution.py:16
  94.4 2.4 collective-permute-done
  97.5 4.4 %collective-permute-start.1 = (bf16[256,512]{1,0:T(8,128)(2,1)S(1)}, bf16[256,512]{1,0:T(8,128)(2,1)S(1)}, u32[]{:S(2)}, u32[]{:S(2)}) collective-permute-start(bf16[256,512]{1,0:T(8,128)(2,1)S(1)} %get-tuple-element.196), channel_id=1, source_target_pairs={{0,4},{4,8},{8,12},{12,16},{16,20},{20,24},{24,28},{1,5},{5,9},{9,... | collective-permute-start | bytes 786440 | tf_op jit(solution)/shard_map/while/body/eval_jaxpr/ppermute | solution.py:16
  101.9 3.7 %collective-permute-start = (bf16[256,512]{1,0:T(8,128)(2,1)S(1)}, bf16[256,512]{1,0:T(8,128)(2,1)S(1)}, u32[]{:S(2)}, u32[]{:S(2)}) collective-permute-start(bf16[256,512]{1,0:T(8,128)(2,1)S(1)} %get-tuple-element.195), channel_id=1, source_target_pairs={{0,4},{4,8},{8,12},{12,16},{16,20},{20,24},{24,28},{1,5},{5,9},{9,... | collective-permute-start | bytes 786440 | tf_op jit(solution)/shard_map/while/body/eval_jaxpr/ppermute | solution.py:16
  106.6 2.4 collective-permute-done
  109.7 4.4 %collective-permute-start.1 = (bf16[256,512]{1,0:T(8,128)(2,1)S(1)}, bf16[256,512]{1,0:T(8,128)(2,1)S(1)}, u32[]{:S(2)}, u32[]{:S(2)}) collective-permute-start(bf16[256,512]{1,0:T(8,128)(2,1)S(1)} %get-tuple-element.196), channel_id=1, source_target_pairs={{0,4},{4,8},{8,12},{12,16},{16,20},{20,24},{24,28},{1,5},{5,9},{9,... | collective-permute-start | bytes 786440 | tf_op jit(solution)/shard_map/while/body/eval_jaxpr/ppermute | solution.py:16
  114.1 3.7 %collective-permute-start = (bf16[256,512]{1,0:T(8,128)(2,1)S(1)}, bf16[256,512]{1,0:T(8,128)(2,1)S(1)}, u32[]{:S(2)}, u32[]{:S(2)}) collective-permute-start(bf16[256,512]{1,0:T(8,128)(2,1)S(1)} %get-tuple-element.195), channel_id=1, source_target_pairs={{0,4},{4,8},{8,12},{12,16},{16,20},{20,24},{24,28},{1,5},{5,9},{9,... | collective-permute-start | bytes 786440 | tf_op jit(solution)/shard_map/while/body/eval_jaxpr/ppermute | solution.py:16
  121.8 4.4 %collective-permute-start.1 = (bf16[256,512]{1,0:T(8,128)(2,1)S(1)}, bf16[256,512]{1,0:T(8,128)(2,1)S(1)}, u32[]{:S(2)}, u32[]{:S(2)}) collective-permute-start(bf16[256,512]{1,0:T(8,128)(2,1)S(1)} %get-tuple-element.196), channel_id=1, source_target_pairs={{0,4},{4,8},{8,12},{12,16},{16,20},{20,24},{24,28},{1,5},{5,9},{9,... | collective-permute-start | bytes 786440 | tf_op jit(solution)/shard_map/while/body/eval_jaxpr/ppermute | solution.py:16
  126.2 3.7 %collective-permute-start = (bf16[256,512]{1,0:T(8,128)(2,1)S(1)}, bf16[256,512]{1,0:T(8,128)(2,1)S(1)}, u32[]{:S(2)}, u32[]{:S(2)}) collective-permute-start(bf16[256,512]{1,0:T(8,128)(2,1)S(1)} %get-tuple-element.195), channel_id=1, source_target_pairs={{0,4},{4,8},{8,12},{12,16},{16,20},{20,24},{24,28},{1,5},{5,9},{9,... | collective-permute-start | bytes 786440 | tf_op jit(solution)/shard_map/while/body/eval_jaxpr/ppermute | solution.py:16
  130.8 2.4 collective-permute-done
  134.0 4.4 %collective-permute-start.1 = (bf16[256,512]{1,0:T(8,128)(2,1)S(1)}, bf16[256,512]{1,0:T(8,128)(2,1)S(1)}, u32[]{:S(2)}, u32[]{:S(2)}) collective-permute-start(bf16[256,512]{1,0:T(8,128)(2,1)S(1)} %get-tuple-element.196), channel_id=1, source_target_pairs={{0,4},{4,8},{8,12},{12,16},{16,20},{20,24},{24,28},{1,5},{5,9},{9,... | collective-permute-start | bytes 786440 | tf_op jit(solution)/shard_map/while/body/eval_jaxpr/ppermute | solution.py:16
  138.3 3.7 %collective-permute-start = (bf16[256,512]{1,0:T(8,128)(2,1)S(1)}, bf16[256,512]{1,0:T(8,128)(2,1)S(1)}, u32[]{:S(2)}, u32[]{:S(2)}) collective-permute-start(bf16[256,512]{1,0:T(8,128)(2,1)S(1)} %get-tuple-element.195), channel_id=1, source_target_pairs={{0,4},{4,8},{8,12},{12,16},{16,20},{20,24},{24,28},{1,5},{5,9},{9,... | collective-permute-start | bytes 786440 | tf_op jit(solution)/shard_map/while/body/eval_jaxpr/ppermute | solution.py:16
  146.1 4.4 %collective-permute-start.1 = (bf16[256,512]{1,0:T(8,128)(2,1)S(1)}, bf16[256,512]{1,0:T(8,128)(2,1)S(1)}, u32[]{:S(2)}, u32[]{:S(2)}) collective-permute-start(bf16[256,512]{1,0:T(8,128)(2,1)S(1)} %get-tuple-element.196), channel_id=1, source_target_pairs={{0,4},{4,8},{8,12},{12,16},{16,20},{20,24},{24,28},{1,5},{5,9},{9,... | collective-permute-start | bytes 786440 | tf_op jit(solution)/shard_map/while/body/eval_jaxpr/ppermute | solution.py:16
  150.5 3.7 %collective-permute-start = (bf16[256,512]{1,0:T(8,128)(2,1)S(1)}, bf16[256,512]{1,0:T(8,128)(2,1)S(1)}, u32[]{:S(2)}, u32[]{:S(2)}) collective-permute-start(bf16[256,512]{1,0:T(8,128)(2,1)S(1)} %get-tuple-element.195), channel_id=1, source_target_pairs={{0,4},{4,8},{8,12},{12,16},{16,20},{20,24},{24,28},{1,5},{5,9},{9,... | collective-permute-start | bytes 786440 | tf_op jit(solution)/shard_map/while/body/eval_jaxpr/ppermute | solution.py:16
  158.2 4.4 %collective-permute-start.1 = (bf16[256,512]{1,0:T(8,128)(2,1)S(1)}, bf16[256,512]{1,0:T(8,128)(2,1)S(1)}, u32[]{:S(2)}, u32[]{:S(2)}) collective-permute-start(bf16[256,512]{1,0:T(8,128)(2,1)S(1)} %get-tuple-element.196), channel_id=1, source_target_pairs={{0,4},{4,8},{8,12},{12,16},{16,20},{20,24},{24,28},{1,5},{5,9},{9,... | collective-permute-start | bytes 786440 | tf_op jit(solution)/shard_map/while/body/eval_jaxpr/ppermute | solution.py:16
  162.6 3.7 %collective-permute-start = (bf16[256,512]{1,0:T(8,128)(2,1)S(1)}, bf16[256,512]{1,0:T(8,128)(2,1)S(1)}, u32[]{:S(2)}, u32[]{:S(2)}) collective-permute-start(bf16[256,512]{1,0:T(8,128)(2,1)S(1)} %get-tuple-element.195), channel_id=1, source_target_pairs={{0,4},{4,8},{8,12},{12,16},{16,20},{20,24},{24,28},{1,5},{5,9},{9,... | collective-permute-start | bytes 786440 | tf_op jit(solution)/shard_map/while/body/eval_jaxpr/ppermute | solution.py:16
  170.4 4.4 %collective-permute-start.1 = (bf16[256,512]{1,0:T(8,128)(2,1)S(1)}, bf16[256,512]{1,0:T(8,128)(2,1)S(1)}, u32[]{:S(2)}, u32[]{:S(2)}) collective-permute-start(bf16[256,512]{1,0:T(8,128)(2,1)S(1)} %get-tuple-element.196), channel_id=1, source_target_pairs={{0,4},{4,8},{8,12},{12,16},{16,20},{20,24},{24,28},{1,5},{5,9},{9,... | collective-permute-start | bytes 786440 | tf_op jit(solution)/shard_map/while/body/eval_jaxpr/ppermute | solution.py:16
  174.8 3.7 %collective-permute-start = (bf16[256,512]{1,0:T(8,128)(2,1)S(1)}, bf16[256,512]{1,0:T(8,128)(2,1)S(1)}, u32[]{:S(2)}, u32[]{:S(2)}) collective-permute-start(bf16[256,512]{1,0:T(8,128)(2,1)S(1)} %get-tuple-element.195), channel_id=1, source_target_pairs={{0,4},{4,8},{8,12},{12,16},{16,20},{20,24},{24,28},{1,5},{5,9},{9,... | collective-permute-start | bytes 786440 | tf_op jit(solution)/shard_map/while/body/eval_jaxpr/ppermute | solution.py:16
  182.5 4.4 %collective-permute-start.1 = (bf16[256,512]{1,0:T(8,128)(2,1)S(1)}, bf16[256,512]{1,0:T(8,128)(2,1)S(1)}, u32[]{:S(2)}, u32[]{:S(2)}) collective-permute-start(bf16[256,512]{1,0:T(8,128)(2,1)S(1)} %get-tuple-element.196), channel_id=1, source_target_pairs={{0,4},{4,8},{8,12},{12,16},{16,20},{20,24},{24,28},{1,5},{5,9},{9,... | collective-permute-start | bytes 786440 | tf_op jit(solution)/shard_map/while/body/eval_jaxpr/ppermute | solution.py:16
  186.9 3.7 %collective-permute-start = (bf16[256,512]{1,0:T(8,128)(2,1)S(1)}, bf16[256,512]{1,0:T(8,128)(2,1)S(1)}, u32[]{:S(2)}, u32[]{:S(2)}) collective-permute-start(bf16[256,512]{1,0:T(8,128)(2,1)S(1)} %get-tuple-element.195), channel_id=1, source_target_pairs={{0,4},{4,8},{8,12},{12,16},{16,20},{20,24},{24,28},{1,5},{5,9},{9,... | collective-permute-start | bytes 786440 | tf_op jit(solution)/shard_map/while/body/eval_jaxpr/ppermute | solution.py:16
  191.6 2.4 collective-permute-done
  194.7 4.4 %collective-permute-start.1 = (bf16[256,512]{1,0:T(8,128)(2,1)S(1)}, bf16[256,512]{1,0:T(8,128)(2,1)S(1)}, u32[]{:S(2)}, u32[]{:S(2)}) collective-permute-start(bf16[256,512]{1,0:T(8,128)(2,1)S(1)} %get-tuple-element.196), channel_id=1, source_target_pairs={{0,4},{4,8},{8,12},{12,16},{16,20},{20,24},{24,28},{1,5},{5,9},{9,... | collective-permute-start | bytes 786440 | tf_op jit(solution)/shard_map/while/body/eval_jaxpr/ppermute | solution.py:16
  199.1 3.7 %collective-permute-start = (bf16[256,512]{1,0:T(8,128)(2,1)S(1)}, bf16[256,512]{1,0:T(8,128)(2,1)S(1)}, u32[]{:S(2)}, u32[]{:S(2)}) collective-permute-start(bf16[256,512]{1,0:T(8,128)(2,1)S(1)} %get-tuple-element.195), channel_id=1, source_target_pairs={{0,4},{4,8},{8,12},{12,16},{16,20},{20,24},{24,28},{1,5},{5,9},{9,... | collective-permute-start | bytes 786440 | tf_op jit(solution)/shard_map/while/body/eval_jaxpr/ppermute | solution.py:16
  206.8 4.4 %collective-permute-start.1 = (bf16[256,512]{1,0:T(8,128)(2,1)S(1)}, bf16[256,512]{1,0:T(8,128)(2,1)S(1)}, u32[]{:S(2)}, u32[]{:S(2)}) collective-permute-start(bf16[256,512]{1,0:T(8,128)(2,1)S(1)} %get-tuple-element.196), channel_id=1, source_target_pairs={{0,4},{4,8},{8,12},{12,16},{16,20},{20,24},{24,28},{1,5},{5,9},{9,... | collective-permute-start | bytes 786440 | tf_op jit(solution)/shard_map/while/body/eval_jaxpr/ppermute | solution.py:16
  211.2 3.7 %collective-permute-start = (bf16[256,512]{1,0:T(8,128)(2,1)S(1)}, bf16[256,512]{1,0:T(8,128)(2,1)S(1)}, u32[]{:S(2)}, u32[]{:S(2)}) collective-permute-start(bf16[256,512]{1,0:T(8,128)(2,1)S(1)} %get-tuple-element.195), channel_id=1, source_target_pairs={{0,4},{4,8},{8,12},{12,16},{16,20},{20,24},{24,28},{1,5},{5,9},{9,... | collective-permute-start | bytes 786440 | tf_op jit(solution)/shard_map/while/body/eval_jaxpr/ppermute | solution.py:16
  219.0 4.4 %collective-permute-start.1 = (bf16[256,512]{1,0:T(8,128)(2,1)S(1)}, bf16[256,512]{1,0:T(8,128)(2,1)S(1)}, u32[]{:S(2)}, u32[]{:S(2)}) collective-permute-start(bf16[256,512]{1,0:T(8,128)(2,1)S(1)} %get-tuple-element.196), channel_id=1, source_target_pairs={{0,4},{4,8},{8,12},{12,16},{16,20},{20,24},{24,28},{1,5},{5,9},{9,... | collective-permute-start | bytes 786440 | tf_op jit(solution)/shard_map/while/body/eval_jaxpr/ppermute | solution.py:16
  223.4 3.7 %collective-permute-start = (bf16[256,512]{1,0:T(8,128)(2,1)S(1)}, bf16[256,512]{1,0:T(8,128)(2,1)S(1)}, u32[]{:S(2)}, u32[]{:S(2)}) collective-permute-start(bf16[256,512]{1,0:T(8,128)(2,1)S(1)} %get-tuple-element.195), channel_id=1, source_target_pairs={{0,4},{4,8},{8,12},{12,16},{16,20},{20,24},{24,28},{1,5},{5,9},{9,... | collective-permute-start | bytes 786440 | tf_op jit(solution)/shard_map/while/body/eval_jaxpr/ppermute | solution.py:16
  231.1 7.8 %fusion.22 = bf16[4096,512]{0,1:T(8,128)(2,1)} fusion(bf16[4096,512]{0,1:T(8,128)(2,1)} %get-tuple-element.124, s32[]{:T(128)S(6)} %select_n.29, bf16[4096,512]{0,1:T(8,128)(2,1)} %copy.62), kind=kLoop, calls=%fused_computation.38 | loop fusion | flops 8388608 | bytes 12582916 | tf_op jit(solution)/shard_map/add | solution.py:83
  238.9 6.4 %fusion.23 = bf16[4096,512]{1,0:T(8,128)(2,1)} fusion(bf16[4096,512]{1,0:T(8,128)(2,1)S(1)} %copy-done.4, s32[]{:T(128)S(6)} %select_n.29, bf16[4096,512]{1,0:T(8,128)(2,1)S(1)} %copy-done.5), kind=kLoop, calls=%fused_computation.39 | loop fusion | flops 8388608 | bytes 12582916 | tf_op jit(solution)/shard_map/add | solution.py:82
  245.8 3.6 %fusion.96 = (f32[2,256]{1,0:T(2,128)S(1)}, f32[2,256,4352]{1,2,0:T(8,128)S(1)}) fusion(bf16[256,2,128]{0,2,1:T(8,128)(2,1)S(1)} %bitcast.117, bf16[4096,512]{1,0:T(8,128)(2,1)} %fusion.23, bf16[256,512]{1,0:T(8,128)(2,1)S(1)} %bitcast.103, pred[256,4352]{0,1:T(8,128)(4,1)S(1)} %fusion.21), kind=kOutput, calls=%fused_computation.95 | convolution fusion | flops 579337728 | bytes 14616576 | tf_op jit(solution)/shard_map/while/body/eval_jaxpr/qgd,kd->gqk/dot_general | solution.py:42
  253.5 3.8 %fusion.95 = (f32[2,256]{1,0:T(2,128)S(1)}, f32[2,256,4352]{1,2,0:T(8,128)S(1)}) fusion(bf16[256,2,128]{0,2,1:T(8,128)(2,1)S(1)} %bitcast.116, bf16[4096,512]{1,0:T(8,128)(2,1)} %fusion.23, bf16[256,512]{1,0:T(8,128)(2,1)S(1)} %bitcast.104, pred[256,4352]{0,1:T(8,128)(4,1)S(1)} %fusion.21), kind=kOutput, calls=%fused_computation.94 | convolution fusion | flops 579337728 | bytes 14616576 | tf_op jit(solution)/shard_map/while/body/eval_jaxpr/qgd,kd->gqk/dot_general | solution.py:42
  261.3 3.6 %fusion.93 = (f32[2,256]{1,0:T(2,128)S(1)}, f32[2,256,4352]{1,2,0:T(8,128)S(1)}) fusion(bf16[256,2,128]{0,2,1:T(8,128)(2,1)S(1)} %bitcast.111, bf16[256,512]{1,0:T(8,128)(2,1)S(1)} %bitcast.105, bf16[4096,512]{1,0:T(8,128)(2,1)} %fusion.23, pred[256,4352]{0,1:T(8,128)(4,1)S(1)} %fusion.21), kind=kOutput, calls=%fused_computation.92 | convolution fusion | flops 579337728 | bytes 14616576 | tf_op jit(solution)/shard_map/while/body/eval_jaxpr/qgd,kd->gqk/dot_general | solution.py:42
  269.0 3.6 %fusion.94 = (f32[2,256]{1,0:T(2,128)S(1)}, f32[2,256,4352]{1,2,0:T(8,128)S(1)}) fusion(bf16[256,2,128]{0,2,1:T(8,128)(2,1)S(1)} %bitcast.115, bf16[4096,512]{1,0:T(8,128)(2,1)} %fusion.23, bf16[256,512]{1,0:T(8,128)(2,1)S(1)} %bitcast.106, pred[256,4352]{0,1:T(8,128)(4,1)S(1)} %fusion.21), kind=kOutput, calls=%fused_computation.93 | convolution fusion | flops 579337728 | bytes 14616576 | tf_op jit(solution)/shard_map/while/body/eval_jaxpr/qgd,kd->gqk/dot_general | solution.py:42
  276.7 16.8 %all_to_all.73 = bf16[4,64,1024]{2,1,0:T(8,128)(2,1)S(1)} all-to-all(bf16[4,64,1024]{2,1,0:T(8,128)(2,1)S(1)} %pad_maximum_fusion.2), channel_id=1, replica_groups=mesh['seq'=8,'head'=4] {'head'}, dimensions={0} | all-to-all | bytes 1048576 | tf_op jit(solution)/shard_map/all_to_all | solution.py:100
  (157 shorter events, 88.2 us)
Async XLA Ops:
  1.7 13.0 %all-to-all-start.1 = ((bf16[64,4,512]{2,0,1:T(8,128)(2,1)}), bf16[64,4,512]{2,0,1:T(8,128)(2,1)S(1)}, u32[]{:S(2)}, u32[]{:S(2)}) async-start(bf16[64,4,512]{2,0,1:T(8,128)(2,1)} %bitcast.99), calls=%async_computation.1 | async-start | bytes 524288 | tf_op jit(solution)/shard_map/all_to_all | solution.py:61
  14.7 15.0 %all-to-all-start = ((bf16[64,4,512]{2,0,1:T(8,128)(2,1)}), bf16[64,4,512]{2,0,1:T(8,128)(2,1)S(1)}, u32[]{:S(2)}, u32[]{:S(2)}) async-start(bf16[64,4,512]{2,0,1:T(8,128)(2,1)} %bitcast.100), calls=%async_computation | async-start | bytes 524288 | tf_op jit(solution)/shard_map/all_to_all | solution.py:60
  29.7 215.6 %all-to-all-start.2 = ((bf16[64,4,1024]{2,0,1:T(8,128)(2,1)}), bf16[64,4,1024]{2,0,1:T(8,128)(2,1)S(1)}, u32[]{:S(2)}, u32[]{:S(2)}) async-start(bf16[64,4,1024]{2,0,1:T(8,128)(2,1)} %bitcast.98), calls=%async_computation.2 | async-start | bytes 1048576 | tf_op jit(solution)/shard_map/all_to_all | solution.py:59
  38.9 9.2 %collective-permute-start.1 = (bf16[256,512]{1,0:T(8,128)(2,1)S(1)}, bf16[256,512]{1,0:T(8,128)(2,1)S(1)}, u32[]{:S(2)}, u32[]{:S(2)}) collective-permute-start(bf16[256,512]{1,0:T(8,128)(2,1)S(1)} %get-tuple-element.196), channel_id=1, source_target_pairs={{0,4},{4,8},{8,12},{12,16},{16,20},{20,24},{24,28},{1,5},{5,9},{9,... | collective-permute-start | bytes 786440 | tf_op jit(solution)/shard_map/while/body/eval_jaxpr/ppermute | solution.py:16
  44.8 6.1 %collective-permute-start = (bf16[256,512]{1,0:T(8,128)(2,1)S(1)}, bf16[256,512]{1,0:T(8,128)(2,1)S(1)}, u32[]{:S(2)}, u32[]{:S(2)}) collective-permute-start(bf16[256,512]{1,0:T(8,128)(2,1)S(1)} %get-tuple-element.195), channel_id=1, source_target_pairs={{0,4},{4,8},{8,12},{12,16},{16,20},{20,24},{24,28},{1,5},{5,9},{9,... | collective-permute-start | bytes 786440 | tf_op jit(solution)/shard_map/while/body/eval_jaxpr/ppermute | solution.py:16
  51.7 7.7 %collective-permute-start.1 = (bf16[256,512]{1,0:T(8,128)(2,1)S(1)}, bf16[256,512]{1,0:T(8,128)(2,1)S(1)}, u32[]{:S(2)}, u32[]{:S(2)}) collective-permute-start(bf16[256,512]{1,0:T(8,128)(2,1)S(1)} %get-tuple-element.196), channel_id=1, source_target_pairs={{0,4},{4,8},{8,12},{12,16},{16,20},{20,24},{24,28},{1,5},{5,9},{9,... | collective-permute-start | bytes 786440 | tf_op jit(solution)/shard_map/while/body/eval_jaxpr/ppermute | solution.py:16
  56.1 6.1 %collective-permute-start = (bf16[256,512]{1,0:T(8,128)(2,1)S(1)}, bf16[256,512]{1,0:T(8,128)(2,1)S(1)}, u32[]{:S(2)}, u32[]{:S(2)}) collective-permute-start(bf16[256,512]{1,0:T(8,128)(2,1)S(1)} %get-tuple-element.195), channel_id=1, source_target_pairs={{0,4},{4,8},{8,12},{12,16},{16,20},{20,24},{24,28},{1,5},{5,9},{9,... | collective-permute-start | bytes 786440 | tf_op jit(solution)/shard_map/while/body/eval_jaxpr/ppermute | solution.py:16
  62.9 7.7 %collective-permute-start.1 = (bf16[256,512]{1,0:T(8,128)(2,1)S(1)}, bf16[256,512]{1,0:T(8,128)(2,1)S(1)}, u32[]{:S(2)}, u32[]{:S(2)}) collective-permute-start(bf16[256,512]{1,0:T(8,128)(2,1)S(1)} %get-tuple-element.196), channel_id=1, source_target_pairs={{0,4},{4,8},{8,12},{12,16},{16,20},{20,24},{24,28},{1,5},{5,9},{9,... | collective-permute-start | bytes 786440 | tf_op jit(solution)/shard_map/while/body/eval_jaxpr/ppermute | solution.py:16
  67.3 6.1 %collective-permute-start = (bf16[256,512]{1,0:T(8,128)(2,1)S(1)}, bf16[256,512]{1,0:T(8,128)(2,1)S(1)}, u32[]{:S(2)}, u32[]{:S(2)}) collective-permute-start(bf16[256,512]{1,0:T(8,128)(2,1)S(1)} %get-tuple-element.195), channel_id=1, source_target_pairs={{0,4},{4,8},{8,12},{12,16},{16,20},{20,24},{24,28},{1,5},{5,9},{9,... | collective-permute-start | bytes 786440 | tf_op jit(solution)/shard_map/while/body/eval_jaxpr/ppermute | solution.py:16
  74.1 7.7 %collective-permute-start.1 = (bf16[256,512]{1,0:T(8,128)(2,1)S(1)}, bf16[256,512]{1,0:T(8,128)(2,1)S(1)}, u32[]{:S(2)}, u32[]{:S(2)}) collective-permute-start(bf16[256,512]{1,0:T(8,128)(2,1)S(1)} %get-tuple-element.196), channel_id=1, source_target_pairs={{0,4},{4,8},{8,12},{12,16},{16,20},{20,24},{24,28},{1,5},{5,9},{9,... | collective-permute-start | bytes 786440 | tf_op jit(solution)/shard_map/while/body/eval_jaxpr/ppermute | solution.py:16
  78.5 6.1 %collective-permute-start = (bf16[256,512]{1,0:T(8,128)(2,1)S(1)}, bf16[256,512]{1,0:T(8,128)(2,1)S(1)}, u32[]{:S(2)}, u32[]{:S(2)}) collective-permute-start(bf16[256,512]{1,0:T(8,128)(2,1)S(1)} %get-tuple-element.195), channel_id=1, source_target_pairs={{0,4},{4,8},{8,12},{12,16},{16,20},{20,24},{24,28},{1,5},{5,9},{9,... | collective-permute-start | bytes 786440 | tf_op jit(solution)/shard_map/while/body/eval_jaxpr/ppermute | solution.py:16
  85.4 8.1 %collective-permute-start.1 = (bf16[256,512]{1,0:T(8,128)(2,1)S(1)}, bf16[256,512]{1,0:T(8,128)(2,1)S(1)}, u32[]{:S(2)}, u32[]{:S(2)}) collective-permute-start(bf16[256,512]{1,0:T(8,128)(2,1)S(1)} %get-tuple-element.196), channel_id=1, source_target_pairs={{0,4},{4,8},{8,12},{12,16},{16,20},{20,24},{24,28},{1,5},{5,9},{9,... | collective-permute-start | bytes 786440 | tf_op jit(solution)/shard_map/while/body/eval_jaxpr/ppermute | solution.py:16
  89.8 7.0 %collective-permute-start = (bf16[256,512]{1,0:T(8,128)(2,1)S(1)}, bf16[256,512]{1,0:T(8,128)(2,1)S(1)}, u32[]{:S(2)}, u32[]{:S(2)}) collective-permute-start(bf16[256,512]{1,0:T(8,128)(2,1)S(1)} %get-tuple-element.195), channel_id=1, source_target_pairs={{0,4},{4,8},{8,12},{12,16},{16,20},{20,24},{24,28},{1,5},{5,9},{9,... | collective-permute-start | bytes 786440 | tf_op jit(solution)/shard_map/while/body/eval_jaxpr/ppermute | solution.py:16
  97.5 8.1 %collective-permute-start.1 = (bf16[256,512]{1,0:T(8,128)(2,1)S(1)}, bf16[256,512]{1,0:T(8,128)(2,1)S(1)}, u32[]{:S(2)}, u32[]{:S(2)}) collective-permute-start(bf16[256,512]{1,0:T(8,128)(2,1)S(1)} %get-tuple-element.196), channel_id=1, source_target_pairs={{0,4},{4,8},{8,12},{12,16},{16,20},{20,24},{24,28},{1,5},{5,9},{9,... | collective-permute-start | bytes 786440 | tf_op jit(solution)/shard_map/while/body/eval_jaxpr/ppermute | solution.py:16
  101.9 7.0 %collective-permute-start = (bf16[256,512]{1,0:T(8,128)(2,1)S(1)}, bf16[256,512]{1,0:T(8,128)(2,1)S(1)}, u32[]{:S(2)}, u32[]{:S(2)}) collective-permute-start(bf16[256,512]{1,0:T(8,128)(2,1)S(1)} %get-tuple-element.195), channel_id=1, source_target_pairs={{0,4},{4,8},{8,12},{12,16},{16,20},{20,24},{24,28},{1,5},{5,9},{9,... | collective-permute-start | bytes 786440 | tf_op jit(solution)/shard_map/while/body/eval_jaxpr/ppermute | solution.py:16
  109.7 8.1 %collective-permute-start.1 = (bf16[256,512]{1,0:T(8,128)(2,1)S(1)}, bf16[256,512]{1,0:T(8,128)(2,1)S(1)}, u32[]{:S(2)}, u32[]{:S(2)}) collective-permute-start(bf16[256,512]{1,0:T(8,128)(2,1)S(1)} %get-tuple-element.196), channel_id=1, source_target_pairs={{0,4},{4,8},{8,12},{12,16},{16,20},{20,24},{24,28},{1,5},{5,9},{9,... | collective-permute-start | bytes 786440 | tf_op jit(solution)/shard_map/while/body/eval_jaxpr/ppermute | solution.py:16
  114.1 7.0 %collective-permute-start = (bf16[256,512]{1,0:T(8,128)(2,1)S(1)}, bf16[256,512]{1,0:T(8,128)(2,1)S(1)}, u32[]{:S(2)}, u32[]{:S(2)}) collective-permute-start(bf16[256,512]{1,0:T(8,128)(2,1)S(1)} %get-tuple-element.195), channel_id=1, source_target_pairs={{0,4},{4,8},{8,12},{12,16},{16,20},{20,24},{24,28},{1,5},{5,9},{9,... | collective-permute-start | bytes 786440 | tf_op jit(solution)/shard_map/while/body/eval_jaxpr/ppermute | solution.py:16
  121.8 8.1 %collective-permute-start.1 = (bf16[256,512]{1,0:T(8,128)(2,1)S(1)}, bf16[256,512]{1,0:T(8,128)(2,1)S(1)}, u32[]{:S(2)}, u32[]{:S(2)}) collective-permute-start(bf16[256,512]{1,0:T(8,128)(2,1)S(1)} %get-tuple-element.196), channel_id=1, source_target_pairs={{0,4},{4,8},{8,12},{12,16},{16,20},{20,24},{24,28},{1,5},{5,9},{9,... | collective-permute-start | bytes 786440 | tf_op jit(solution)/shard_map/while/body/eval_jaxpr/ppermute | solution.py:16
  126.2 7.0 %collective-permute-start = (bf16[256,512]{1,0:T(8,128)(2,1)S(1)}, bf16[256,512]{1,0:T(8,128)(2,1)S(1)}, u32[]{:S(2)}, u32[]{:S(2)}) collective-permute-start(bf16[256,512]{1,0:T(8,128)(2,1)S(1)} %get-tuple-element.195), channel_id=1, source_target_pairs={{0,4},{4,8},{8,12},{12,16},{16,20},{20,24},{24,28},{1,5},{5,9},{9,... | collective-permute-start | bytes 786440 | tf_op jit(solution)/shard_map/while/body/eval_jaxpr/ppermute | solution.py:16
  134.0 8.1 %collective-permute-start.1 = (bf16[256,512]{1,0:T(8,128)(2,1)S(1)}, bf16[256,512]{1,0:T(8,128)(2,1)S(1)}, u32[]{:S(2)}, u32[]{:S(2)}) collective-permute-start(bf16[256,512]{1,0:T(8,128)(2,1)S(1)} %get-tuple-element.196), channel_id=1, source_target_pairs={{0,4},{4,8},{8,12},{12,16},{16,20},{20,24},{24,28},{1,5},{5,9},{9,... | collective-permute-start | bytes 786440 | tf_op jit(solution)/shard_map/while/body/eval_jaxpr/ppermute | solution.py:16
  138.3 7.0 %collective-permute-start = (bf16[256,512]{1,0:T(8,128)(2,1)S(1)}, bf16[256,512]{1,0:T(8,128)(2,1)S(1)}, u32[]{:S(2)}, u32[]{:S(2)}) collective-permute-start(bf16[256,512]{1,0:T(8,128)(2,1)S(1)} %get-tuple-element.195), channel_id=1, source_target_pairs={{0,4},{4,8},{8,12},{12,16},{16,20},{20,24},{24,28},{1,5},{5,9},{9,... | collective-permute-start | bytes 786440 | tf_op jit(solution)/shard_map/while/body/eval_jaxpr/ppermute | solution.py:16
  146.1 8.1 %collective-permute-start.1 = (bf16[256,512]{1,0:T(8,128)(2,1)S(1)}, bf16[256,512]{1,0:T(8,128)(2,1)S(1)}, u32[]{:S(2)}, u32[]{:S(2)}) collective-permute-start(bf16[256,512]{1,0:T(8,128)(2,1)S(1)} %get-tuple-element.196), channel_id=1, source_target_pairs={{0,4},{4,8},{8,12},{12,16},{16,20},{20,24},{24,28},{1,5},{5,9},{9,... | collective-permute-start | bytes 786440 | tf_op jit(solution)/shard_map/while/body/eval_jaxpr/ppermute | solution.py:16
  150.5 7.0 %collective-permute-start = (bf16[256,512]{1,0:T(8,128)(2,1)S(1)}, bf16[256,512]{1,0:T(8,128)(2,1)S(1)}, u32[]{:S(2)}, u32[]{:S(2)}) collective-permute-start(bf16[256,512]{1,0:T(8,128)(2,1)S(1)} %get-tuple-element.195), channel_id=1, source_target_pairs={{0,4},{4,8},{8,12},{12,16},{16,20},{20,24},{24,28},{1,5},{5,9},{9,... | collective-permute-start | bytes 786440 | tf_op jit(solution)/shard_map/while/body/eval_jaxpr/ppermute | solution.py:16
  158.2 8.1 %collective-permute-start.1 = (bf16[256,512]{1,0:T(8,128)(2,1)S(1)}, bf16[256,512]{1,0:T(8,128)(2,1)S(1)}, u32[]{:S(2)}, u32[]{:S(2)}) collective-permute-start(bf16[256,512]{1,0:T(8,128)(2,1)S(1)} %get-tuple-element.196), channel_id=1, source_target_pairs={{0,4},{4,8},{8,12},{12,16},{16,20},{20,24},{24,28},{1,5},{5,9},{9,... | collective-permute-start | bytes 786440 | tf_op jit(solution)/shard_map/while/body/eval_jaxpr/ppermute | solution.py:16
  162.6 7.0 %collective-permute-start = (bf16[256,512]{1,0:T(8,128)(2,1)S(1)}, bf16[256,512]{1,0:T(8,128)(2,1)S(1)}, u32[]{:S(2)}, u32[]{:S(2)}) collective-permute-start(bf16[256,512]{1,0:T(8,128)(2,1)S(1)} %get-tuple-element.195), channel_id=1, source_target_pairs={{0,4},{4,8},{8,12},{12,16},{16,20},{20,24},{24,28},{1,5},{5,9},{9,... | collective-permute-start | bytes 786440 | tf_op jit(solution)/shard_map/while/body/eval_jaxpr/ppermute | solution.py:16
  170.4 8.1 %collective-permute-start.1 = (bf16[256,512]{1,0:T(8,128)(2,1)S(1)}, bf16[256,512]{1,0:T(8,128)(2,1)S(1)}, u32[]{:S(2)}, u32[]{:S(2)}) collective-permute-start(bf16[256,512]{1,0:T(8,128)(2,1)S(1)} %get-tuple-element.196), channel_id=1, source_target_pairs={{0,4},{4,8},{8,12},{12,16},{16,20},{20,24},{24,28},{1,5},{5,9},{9,... | collective-permute-start | bytes 786440 | tf_op jit(solution)/shard_map/while/body/eval_jaxpr/ppermute | solution.py:16
  174.8 7.0 %collective-permute-start = (bf16[256,512]{1,0:T(8,128)(2,1)S(1)}, bf16[256,512]{1,0:T(8,128)(2,1)S(1)}, u32[]{:S(2)}, u32[]{:S(2)}) collective-permute-start(bf16[256,512]{1,0:T(8,128)(2,1)S(1)} %get-tuple-element.195), channel_id=1, source_target_pairs={{0,4},{4,8},{8,12},{12,16},{16,20},{20,24},{24,28},{1,5},{5,9},{9,... | collective-permute-start | bytes 786440 | tf_op jit(solution)/shard_map/while/body/eval_jaxpr/ppermute | solution.py:16
  182.5 8.1 %collective-permute-start.1 = (bf16[256,512]{1,0:T(8,128)(2,1)S(1)}, bf16[256,512]{1,0:T(8,128)(2,1)S(1)}, u32[]{:S(2)}, u32[]{:S(2)}) collective-permute-start(bf16[256,512]{1,0:T(8,128)(2,1)S(1)} %get-tuple-element.196), channel_id=1, source_target_pairs={{0,4},{4,8},{8,12},{12,16},{16,20},{20,24},{24,28},{1,5},{5,9},{9,... | collective-permute-start | bytes 786440 | tf_op jit(solution)/shard_map/while/body/eval_jaxpr/ppermute | solution.py:16
  186.9 7.0 %collective-permute-start = (bf16[256,512]{1,0:T(8,128)(2,1)S(1)}, bf16[256,512]{1,0:T(8,128)(2,1)S(1)}, u32[]{:S(2)}, u32[]{:S(2)}) collective-permute-start(bf16[256,512]{1,0:T(8,128)(2,1)S(1)} %get-tuple-element.195), channel_id=1, source_target_pairs={{0,4},{4,8},{8,12},{12,16},{16,20},{20,24},{24,28},{1,5},{5,9},{9,... | collective-permute-start | bytes 786440 | tf_op jit(solution)/shard_map/while/body/eval_jaxpr/ppermute | solution.py:16
  194.7 8.1 %collective-permute-start.1 = (bf16[256,512]{1,0:T(8,128)(2,1)S(1)}, bf16[256,512]{1,0:T(8,128)(2,1)S(1)}, u32[]{:S(2)}, u32[]{:S(2)}) collective-permute-start(bf16[256,512]{1,0:T(8,128)(2,1)S(1)} %get-tuple-element.196), channel_id=1, source_target_pairs={{0,4},{4,8},{8,12},{12,16},{16,20},{20,24},{24,28},{1,5},{5,9},{9,... | collective-permute-start | bytes 786440 | tf_op jit(solution)/shard_map/while/body/eval_jaxpr/ppermute | solution.py:16
  199.1 7.0 %collective-permute-start = (bf16[256,512]{1,0:T(8,128)(2,1)S(1)}, bf16[256,512]{1,0:T(8,128)(2,1)S(1)}, u32[]{:S(2)}, u32[]{:S(2)}) collective-permute-start(bf16[256,512]{1,0:T(8,128)(2,1)S(1)} %get-tuple-element.195), channel_id=1, source_target_pairs={{0,4},{4,8},{8,12},{12,16},{16,20},{20,24},{24,28},{1,5},{5,9},{9,... | collective-permute-start | bytes 786440 | tf_op jit(solution)/shard_map/while/body/eval_jaxpr/ppermute | solution.py:16
  206.8 8.1 %collective-permute-start.1 = (bf16[256,512]{1,0:T(8,128)(2,1)S(1)}, bf16[256,512]{1,0:T(8,128)(2,1)S(1)}, u32[]{:S(2)}, u32[]{:S(2)}) collective-permute-start(bf16[256,512]{1,0:T(8,128)(2,1)S(1)} %get-tuple-element.196), channel_id=1, source_target_pairs={{0,4},{4,8},{8,12},{12,16},{16,20},{20,24},{24,28},{1,5},{5,9},{9,... | collective-permute-start | bytes 786440 | tf_op jit(solution)/shard_map/while/body/eval_jaxpr/ppermute | solution.py:16
  211.2 7.0 %collective-permute-start = (bf16[256,512]{1,0:T(8,128)(2,1)S(1)}, bf16[256,512]{1,0:T(8,128)(2,1)S(1)}, u32[]{:S(2)}, u32[]{:S(2)}) collective-permute-start(bf16[256,512]{1,0:T(8,128)(2,1)S(1)} %get-tuple-element.195), channel_id=1, source_target_pairs={{0,4},{4,8},{8,12},{12,16},{16,20},{20,24},{24,28},{1,5},{5,9},{9,... | collective-permute-start | bytes 786440 | tf_op jit(solution)/shard_map/while/body/eval_jaxpr/ppermute | solution.py:16
  219.0 8.1 %collective-permute-start.1 = (bf16[256,512]{1,0:T(8,128)(2,1)S(1)}, bf16[256,512]{1,0:T(8,128)(2,1)S(1)}, u32[]{:S(2)}, u32[]{:S(2)}) collective-permute-start(bf16[256,512]{1,0:T(8,128)(2,1)S(1)} %get-tuple-element.196), channel_id=1, source_target_pairs={{0,4},{4,8},{8,12},{12,16},{16,20},{20,24},{24,28},{1,5},{5,9},{9,... | collective-permute-start | bytes 786440 | tf_op jit(solution)/shard_map/while/body/eval_jaxpr/ppermute | solution.py:16
  223.4 7.0 %collective-permute-start = (bf16[256,512]{1,0:T(8,128)(2,1)S(1)}, bf16[256,512]{1,0:T(8,128)(2,1)S(1)}, u32[]{:S(2)}, u32[]{:S(2)}) collective-permute-start(bf16[256,512]{1,0:T(8,128)(2,1)S(1)} %get-tuple-element.195), channel_id=1, source_target_pairs={{0,4},{4,8},{8,12},{12,16},{16,20},{20,24},{24,28},{1,5},{5,9},{9,... | collective-permute-start | bytes 786440 | tf_op jit(solution)/shard_map/while/body/eval_jaxpr/ppermute | solution.py:16
  231.1 7.8 %copy-start.4 = (bf16[4096,512]{1,0:T(8,128)(2,1)S(1)}, bf16[4096,512]{1,0:T(8,128)(2,1)}, u32[]{:S(2)}) copy-start(bf16[4096,512]{1,0:T(8,128)(2,1)} %get-tuple-element.125) | copy-start | bytes 12582916
  231.1 7.8 %copy-start.5 = (bf16[4096,512]{1,0:T(8,128)(2,1)S(1)}, bf16[4096,512]{1,0:T(8,128)(2,1)}, u32[]{:S(2)}) copy-start(bf16[4096,512]{1,0:T(8,128)(2,1)} %param.11) | copy-start | bytes 12582916
  249.5 2.2 copy-start
  257.3 2.2 copy-start.1
  264.9 2.2 copy-start.2
  272.6 2.2 copy-start.3
where the time goes:
time: 300 us; the launch traced here: 294 us
  starting transfers between devices  138 us (46%)
  local copies, waits for them, and re-layouts  48.9 us (16%)
  waiting for transfers between devices  45.7 us (15%)
  other arithmetic  22.2 us (7%)
  matrix products  21.1 us (7%)
  blocking collectives  16.8 us (6%)
    ppermute x32, starting transfers between devices, shifted(): return lax.ppermute(shard, axis, pairs)  125 us
    ppermute x32, waiting for transfers between devices, shifted(): return lax.ppermute(shard, axis, pairs)  40.5 us
    all_to_all x1, blocking collectives, shards(): lax.all_to_all(shortened(attended), 'head', split_axis=0, concat_axis=1,...  16.8 us
    dot_general x4, matrix products, attend_block(): jnp.einsum('qgd,kd->gqk', query_head, key_head, preferred_element_type=jn...  14.6 us
    dynamic_update_slice x32, local copies, waits for them, and re-layouts, relay(): lax.dynamic_update_slice_in_dim(window_values, moving_values, offset, 0)  14.1 us
    dynamic_update_slice x16, local copies, waits for them, and re-layouts, relay(): lax.dynamic_update_slice_in_dim(window_keys, moving_keys, offset, 0)  11.7 us
    unnamed x14, local copies, waits for them, and re-layouts  10.4 us
    add x1, other arithmetic, shards(): window_values + lax.dynamic_slice_in_dim(padded_values, first_row, WINDOW...  7.84 us
  transfers between devices with their start and end apart: 35, of which 21 were waited for; matrix products, arithmetic and copies ran while one was open for 20% of the time, Pallas kernels for 0%

commit v1 on v0

--- a/solution.py
+++ b/solution.py
@@ -1,6 +1,10 @@
+import functools
+
 import jax
 import jax.numpy as jnp
 from jax import lax
+from jax.experimental import pallas as pl
+from jax.experimental.pallas import tpu as pltpu
 from jax.sharding import PartitionSpec as P
 
 HEAD_DIM = 128
@@ -8,6 +12,13 @@
 KVH = 16
 QSCALE = 144
 WINDOW = 4096
+GROUPING = QH // KVH
+EXP2_SCALE = 1.4426950408889634 * QSCALE**-0.5
+LOWEST = -1e30
+ONES_ROWS = 16
+V_ROWS = HEAD_DIM + ONES_ROWS
+PREFIX_TILE = 1024
+SPAN_TILE = 1024
 
 
 def shifted(shard, axis, by):
@@ -54,7 +65,7 @@
     return jnp.concatenate(outputs, axis=1).astype(jnp.bfloat16)
 
 
-def shards(queries, keys, values, prefix_keys, prefix_values, span_start):
+def relayed_shards(queries, keys, values, prefix_keys, prefix_values, span_start):
     query_local, key_local, value_local = (
         lax.all_to_all(queries, "head", split_axis=1, concat_axis=0, tiled=True),
         lax.all_to_all(keys, "head", split_axis=1, concat_axis=0, tiled=True),
@@ -102,6 +113,345 @@
     ).astype(attended.dtype)
 
 
+def in_vmem():
+    return pl.BlockSpec(memory_space=pltpu.VMEM)
+
+
+def in_smem():
+    return pl.BlockSpec(memory_space=pltpu.SMEM)
+
+
+def anywhere():
+    return pl.BlockSpec(memory_space=pl.ANY)
+
+
+def params():
+    return pltpu.CompilerParams(vmem_limit_bytes=40 * 2**20)
+
+
+def lanes(index, width):
+    return pl.ds(pl.multiple_of(index * width, width), width)
+
+
+def split_planes(queries, keys, values):
+    rows = queries.shape[0]
+    planes = lax.axis_size("head")
+    q_width, kv_width = queries.shape[1] // planes, keys.shape[1] // planes
+
+    def kernel(q_ref, k_ref, v_ref, *rest):
+        kv_out, q_out, sems = rest[:planes], rest[planes : 2 * planes], rest[2 * planes]
+        here = lax.axis_index("head")
+        copies = []
+        for r in range(planes):
+            plane = here ^ r
+            for source, width, target in (
+                (k_ref, kv_width, kv_out[r].at[:, pl.ds(0, kv_width)]),
+                (v_ref, kv_width, kv_out[r].at[:, pl.ds(kv_width, kv_width)]),
+                (q_ref, q_width, q_out[r]),
+            ):
+                copy = pltpu.make_async_copy(
+                    source.at[:, lanes(plane, width)], target, sems.at[len(copies)]
+                )
+                copy.start()
+                copies.append(copy)
+        for copy in copies:
+            copy.wait()
+
+    out = [jax.ShapeDtypeStruct((rows, 2 * kv_width), jnp.bfloat16)] * planes
+    out += [jax.ShapeDtypeStruct((rows, q_width), jnp.bfloat16)] * planes
+    result = pl.pallas_call(
+        kernel,
+        out_shape=out,
+        in_specs=[anywhere()] * 3,
+        out_specs=[in_vmem()] * (2 * planes),
+        scratch_shapes=[pltpu.SemaphoreType.DMA((3 * planes,))],
+        compiler_params=params(),
+        name="split_planes",
+    )(queries, keys, values)
+    return result[:planes], result[planes:]
+
+
+def join_planes(pieces):
+    rows, width = pieces[0].shape
+    planes = len(pieces)
+
+    def kernel(*refs):
+        out_ref, sems = refs[planes], refs[planes + 1]
+        here = lax.axis_index("head")
+        copies = []
+        for r in range(planes):
+            copy = pltpu.make_async_copy(
+                refs[r], out_ref.at[:, lanes(here ^ r, width)], sems.at[r]
+            )
+            copy.start()
+            copies.append(copy)
+        for copy in copies:
+            copy.wait()
+
+    return pl.pallas_call(
+        kernel,
+        out_shape=jax.ShapeDtypeStruct((rows, planes * width), jnp.bfloat16),
+        in_specs=[in_vmem()] * planes,
+        out_specs=anywhere(),
+        scratch_shapes=[pltpu.SemaphoreType.DMA((planes,))],
+        compiler_params=params(),
+        name="join_planes",
+    )(*pieces)
+
+
+def turn_prefix_values(prefix_values):
+    count, width = prefix_values.shape
+    heads = width // HEAD_DIM
+
+    def kernel(v_ref, out_ref):
+        out_ref[:, HEAD_DIM:, :] = jnp.ones((heads, ONES_ROWS, count), jnp.bfloat16)
+
+        def turn(chunk, _):
+            at = lanes(chunk, 512)
+            for g in range(heads):
+                out_ref[g, :HEAD_DIM, at] = v_ref[at, g * HEAD_DIM : (g + 1) * HEAD_DIM].T
+            return 0
+
+        lax.fori_loop(0, count // 512, turn, 0)
+
+    return pl.pallas_call(
+        kernel,
+        out_shape=jax.ShapeDtypeStruct((heads, V_ROWS, count), jnp.bfloat16),
+        in_specs=[in_vmem()],
+        out_specs=in_vmem(),
+        compiler_params=params(),
+        cost_estimate=pl.CostEstimate(flops=0, bytes_accessed=2**23, transcendentals=0),
+        name="turn_prefix_values",
+    )(prefix_values)
+
+
+def stack_pair(first, second):
+    rows, width = first.shape
+    heads = width // (2 * HEAD_DIM)
+
+    def kernel(a_ref, b_ref, out_ref):
+        for g in range(2 * heads):
+            at = slice(g * HEAD_DIM, (g + 1) * HEAD_DIM)
+            both = jnp.concatenate([a_ref[:, at], b_ref[:, at]], axis=0)
+            out_ref[g] = both if g < heads else both.T
+
+    return pl.pallas_call(
+        kernel,
+        out_shape=jax.ShapeDtypeStruct((2 * heads, 2 * rows, HEAD_DIM), jnp.bfloat16),
+        in_specs=[in_vmem()] * 2,
+        out_specs=in_vmem(),
+        compiler_params=params(),
+        cost_estimate=pl.CostEstimate(flops=0, bytes_accessed=2**21, transcendentals=0),
+        name="stack_pair",
+    )(first, second)
+
+
+def tile_of_heads(heads, scores_of, values_of, allowed, m_ref, acc_ref, opening):
+    scores = scores_of(0)
+    for g in range(heads):
+        now = scores
+        if g + 1 < heads:
+            scores = scores_of(g + 1)
+        if allowed is not None:
+            now = jnp.where(allowed, now, -jnp.inf)
+        peak = jnp.max(now, axis=0, keepdims=True)
+        before = None if opening else m_ref[g, :1, :]
+        peak = jnp.maximum(peak, LOWEST if opening else before)
+        scaled = peak * EXP2_SCALE
+        weights = jnp.exp2(now * EXP2_SCALE - scaled).astype(jnp.bfloat16)
+        sums = jnp.dot(values_of(g), weights, preferred_element_type=jnp.float32)
+        if not opening:
+            sums = sums + acc_ref[g] * jnp.exp2(before * EXP2_SCALE - scaled)
+        acc_ref[g] = sums
+        m_ref[g] = jnp.broadcast_to(peak, m_ref.shape[1:])
+
+
+def dot_turned(keys, queries):
+    return lax.dot_general(
+        keys, queries, (((1,), (1,)), ((), ())), preferred_element_type=jnp.float32
+    )
+
+
+def attend_prefix(span_start, pieces, prefix_keys, turned_values):
+    rows, width = pieces[0].shape
+    planes = len(pieces)
+    window = prefix_keys.shape[0]
+    heads = prefix_keys.shape[1] // HEAD_DIM
+    block = planes * rows
+    columns = GROUPING * block
+    size = PREFIX_TILE
+
+    def kernel(start_ref, *refs):
+        q_refs = refs[:planes]
+        k_ref, v_ref, q_all, m_ref, acc_ref = refs[planes:]
+        for r in range(planes):
+            for h in range(heads * GROUPING):
+                at = (h % GROUPING) * block + r * rows
+                q_all[h // GROUPING, at : at + rows, :] = q_refs[r][
+                    :, h * HEAD_DIM : (h + 1) * HEAD_DIM
+                ]
+        first_query = lax.axis_index("seq") * block
+        turn = lax.axis_index("head") * rows
+        first_key = window - start_ref[0]
+        lowest = jnp.maximum(first_query + 1, first_key)
+        tiles = (window - lowest + size - 1) // size
+
+        def tile(j, masked):
+            row = pl.multiple_of(window - (j + 1) * size, size)
+            allowed = None
+            if masked:
+                key = lax.broadcasted_iota(jnp.int32, (size, columns), 0)
+                place = lax.broadcasted_iota(jnp.int32, (1, columns), 1) % block
+                query = first_query + (place ^ turn)
+                allowed = key >= jnp.maximum(query + 1, first_key) - row
+            tile_of_heads(
+                heads,
+                lambda g: dot_turned(
+                    k_ref[pl.ds(row, size), g * HEAD_DIM : (g + 1) * HEAD_DIM], q_all[g]
+                ),
+                lambda g: v_ref[g, :, pl.ds(row, size)],
+                allowed,
+                m_ref,
+                acc_ref,
+                masked,
+            )
+
+        @pl.when(tiles == 0)
+        def _():
+            m_ref[...] = jnp.full(m_ref.shape, LOWEST, jnp.float32)
+            acc_ref[...] = jnp.zeros(acc_ref.shape, jnp.float32)
+
+        @pl.when(tiles > 0)
+        def _():
+            tile(tiles - 1, True)
+
+        def one(j, _):
+            tile(j, False)
+            return 0
+
+        lax.fori_loop(0, tiles - 1, one, 0)
+
+    return pl.pallas_call(
+        kernel,
+        out_shape=[
+            jax.ShapeDtypeStruct((heads, columns, HEAD_DIM), jnp.bfloat16),
+            jax.ShapeDtypeStruct((heads, 8, columns), jnp.float32),
+            jax.ShapeDtypeStruct((heads, V_ROWS, columns), jnp.float32),
+        ],
+        in_specs=[in_smem()] + [in_vmem()] * (planes + 2),
+        out_specs=[in_vmem()] * 3,
+        compiler_params=params(),
+        cost_estimate=pl.CostEstimate(
+            flops=4 * heads * columns * window * HEAD_DIM, bytes_accessed=2**23,
+            transcendentals=heads * columns * window
+        ),
+        name="attend_prefix",
+    )(span_start, *pieces, prefix_keys, turned_values)
+
+
+def attend_span(q_all, m, acc, sources):
+    heads, columns, _ = q_all.shape
+    block = columns // GROUPING
+    half_rows = sources[0][0].shape[1]
+    halves = block // half_rows
+    blocks = len(sources)
+    tokens = blocks * block
+    planes = lax.axis_size("head")
+    rows = block // planes
+    size = min(SPAN_TILE, tokens)
+    flat = [piece for source in sources for piece in source]
+
+    def kernel(q_ref, m_in, acc_in, *refs):
+        kv_refs = refs[: len(flat)]
+        o_refs = refs[len(flat) : len(flat) + planes]
+        m_ref, acc_ref, k_all, v_all = refs[len(flat) + planes :]
+        me = lax.axis_index("seq")
+        turn = lax.axis_index("head") * rows
+        m_ref[...] = m_in[...]
+        acc_ref[...] = acc_in[...]
+        v_all[:, HEAD_DIM:, :] = jnp.ones((heads, ONES_ROWS, tokens), jnp.bfloat16)
+        for index, piece in enumerate(kv_refs):
+            at = lanes((me ^ (index // halves)) * halves + index % halves, half_rows)
+            for g in range(heads):
+                k_all[g, at, :] = piece[g]
+                v_all[g, :HEAD_DIM, at] = piece[heads + g]
+        last = me * block // size
+
+        def tile(j, masked):
+            row = pl.multiple_of(j * size, size)
+            allowed = None
+            if masked:
+                key = row + lax.broadcasted_iota(jnp.int32, (size, 1), 0)
+                place = lax.broadcasted_iota(jnp.int32, (1, columns), 1) % block
+                allowed = (key ^ turn) <= me * block + (place ^ turn)
+            tile_of_heads(
+                heads,
+                lambda g: dot_turned(k_all[g, pl.ds(row, size), :], q_ref[g]),
+                lambda g: v_all[g, :, pl.ds(row, size)],
+                allowed,
+                m_ref,
+                acc_ref,
+                False,
+            )
+
+        tile(last, True)
+
+        def one(j, _):
+            tile(j, False)
+            return 0
+
+        lax.fori_loop(0, last, one, 0)
+        for g in range(heads):
+            mixed = acc_ref[g, :HEAD_DIM, :] / acc_ref[g, HEAD_DIM : HEAD_DIM + 1, :]
+            mixed = mixed.T.astype(jnp.bfloat16)
+            for e in range(GROUPING):
+                for r in range(planes):
+                    at = e * block + r * rows
+                    h = g * GROUPING + e
+                    o_refs[r][:, h * HEAD_DIM : (h + 1) * HEAD_DIM] = mixed[at : at + rows]
+
+    out = jax.ShapeDtypeStruct((rows, heads * GROUPING * HEAD_DIM), jnp.bfloat16)
+    return pl.pallas_call(
+        kernel,
+        out_shape=[out] * planes,
+        in_specs=[in_vmem()] * (3 + len(flat)),
+        out_specs=[in_vmem()] * planes,
+        scratch_shapes=[
+            pltpu.VMEM(m.shape, jnp.float32),
+            pltpu.VMEM(acc.shape, jnp.float32),
+            pltpu.VMEM((heads, tokens, HEAD_DIM), jnp.bfloat16),
+            pltpu.VMEM((heads, V_ROWS, tokens), jnp.bfloat16),
+        ],
+        compiler_params=params(),
+        cost_estimate=pl.CostEstimate(
+            flops=4 * heads * columns * tokens * HEAD_DIM, bytes_accessed=2**22,
+            transcendentals=heads * columns * tokens
+        ),
+        name="attend_span",
+    )(q_all, m, acc, *flat)
+
+
+def swapped(shard, axis, bits):
+    return lax.ppermute(shard, axis, [(i, i ^ bits) for i in range(lax.axis_size(axis))])
+
+
+def gathered_shards(queries, keys, values, prefix_keys, prefix_values, span_start):
+    planes = lax.axis_size("head")
+    blocks = lax.axis_size("seq")
+    kv, q = split_planes(queries, keys, values)
+    kv = [kv[0]] + [swapped(kv[r], "head", r) for r in range(1, planes)]
+    q = [q[0]] + [swapped(q[r], "head", r) for r in range(1, planes)]
+    turned = turn_prefix_values(prefix_values)
+    halves = [stack_pair(kv[r], kv[r + 1]) for r in range(0, planes, 2)]
+    near = [halves] + [[swapped(h, "seq", c) for h in halves] for c in range(2, blocks, 2)]
+    far = [[swapped(h, "seq", 1) for h in source] for source in near]
+    sources = [source for couple in zip(near, far) for source in couple]
+    q_all, m, acc = attend_prefix(span_start, q, prefix_keys, turned)
+    pieces = attend_span(q_all, m, acc, sources)
+    pieces = [pieces[0]] + [swapped(pieces[r], "head", r) for r in range(1, planes)]
+    return join_planes(pieces)
+
+
 def solution(mesh):
     placed = (
         P(("seq", "head"), None),
@@ -111,6 +461,8 @@
         P(None, "head"),
         P(),
     )
+    fits = mesh.shape["seq"] == 8 and mesh.shape["head"] == 4
+    shards = gathered_shards if fits else relayed_shards
     return jax.shard_map(
         shards, mesh=mesh, in_specs=placed, out_specs=P(("seq", "head"), None), check_vma=False
     )

time: 300 us -> 82.8 us (0.28)
  the two profiles are of different devices: /device:TPU:1 before, /device:TPU:20 now
where the time goes in v1:
time: 82.8 us; the launch traced here: 82.1 us
  waiting for transfers between devices  33.3 us (40%)
  Pallas kernels  21.8 us (26%)
  starting transfers between devices  20.9 us (25%)
  local copies, waits for them, and re-layouts  5.13 us (6%)
  between operations  0.92 us (1%)
    ppermute x23, waiting for transfers between devices, swapped(): lax.ppermute(shard, axis, [(i, i ^ bits) for i in range(lax.axis_size(axi...  33.3 us
    ppermute x23, starting transfers between devices, swapped(): lax.ppermute(shard, axis, [(i, i ^ bits) for i in range(lax.axis_size(axi...  20.9 us
    pallas_call x1, Pallas kernels, attend_prefix(): pl.pallas_call(kernel, out_shape=[jax.ShapeDtypeStruct((heads, columns, H...  11 us
    pallas_call x1, Pallas kernels, attend_span(): pl.pallas_call(kernel, out_shape=[out] * planes, in_specs=[in_vmem()] * (...  7.98 us
    unnamed x10, local copies, waits for them, and re-layouts  5.13 us
  transfers between devices with their start and end apart: 23, of which 9 were waited for; matrix products, arithmetic and copies ran while one was open for 0% of the time, Pallas kernels for 15%

profile of v1, /device:TPU:20, one launch (start us, length us, event | category | flops | bytes accessed | tf_op | source)
XLA Modules:
  0.0 82.1 jit_solution(16853536487655657407)
XLA Ops:
  0.0 1.0 %copy-done.1 = bf16[64,4096]{1,0:T(8,128)(2,1)S(1)} copy-done((bf16[64,4096]{1,0:T(8,128)(2,1)S(1)}, bf16[64,4096]{1,0:T(8,128)(2,1)}, u32[]{:S(2)}) %copy-start.1) | copy-done | bytes 524312
  1.0 0.9 %copy-done.2 = bf16[64,2048]{1,0:T(8,128)(2,1)S(1)} copy-done((bf16[64,2048]{1,0:T(8,128)(2,1)S(1)}, bf16[64,2048]{1,0:T(8,128)(2,1)}, u32[]{:S(2)}) %copy-start.2) | copy-done | bytes 262168
  2.0 0.9 %copy-done.3 = bf16[64,2048]{1,0:T(8,128)(2,1)S(1)} copy-done((bf16[64,2048]{1,0:T(8,128)(2,1)S(1)}, bf16[64,2048]{1,0:T(8,128)(2,1)}, u32[]{:S(2)}) %copy-start.3) | copy-done | bytes 262168
  2.9 0.3 split_planes.1
  3.3 0.4 collective-permute-start.4
  3.7 2.7 %collective-permute-start.5 = (bf16[64,1024]{1,0:T(8,128)(2,1)S(1)}, bf16[64,1024]{1,0:T(8,128)(2,1)S(1)}, u32[]{:S(2)}, u32[]{:S(2)}) collective-permute-start(bf16[64,1024]{1,0:T(8,128)(2,1)S(1)} %get-tuple-element.30), channel_id=1, source_target_pairs={{0,3},{1,2},{2,1},{3,0},{4,7},{5,6},{6,5},{7,4},{8,11},{9,10},{10,... | collective-permute-start | bytes 393224 | tf_op jit(solution)/shard_map/ppermute | solution.py:435
  6.4 1.3 %collective-permute-start.3 = (bf16[64,1024]{1,0:T(8,128)(2,1)S(1)}, bf16[64,1024]{1,0:T(8,128)(2,1)S(1)}, u32[]{:S(2)}, u32[]{:S(2)}) collective-permute-start(bf16[64,1024]{1,0:T(8,128)(2,1)S(1)} %get-tuple-element.28), channel_id=1, source_target_pairs={{0,1},{1,0},{2,3},{3,2},{4,5},{5,4},{6,7},{7,6},{8,9},{9,8},{10,11... | collective-permute-start | bytes 393224 | tf_op jit(solution)/shard_map/ppermute | solution.py:435
  7.7 0.7 collective-permute-start
  8.4 1.2 %collective-permute-start.1 = (bf16[64,1024]{1,0:T(8,128)(2,1)S(1)}, bf16[64,1024]{1,0:T(8,128)(2,1)S(1)}, u32[]{:S(2)}, u32[]{:S(2)}) collective-permute-start(bf16[64,1024]{1,0:T(8,128)(2,1)S(1)} %get-tuple-element.22), channel_id=1, source_target_pairs={{0,2},{1,3},{2,0},{3,1},{4,6},{5,7},{6,4},{7,5},{8,10},{9,11},{10,... | collective-permute-start | bytes 393224 | tf_op jit(solution)/shard_map/ppermute | solution.py:435
  9.6 3.6 %collective-permute-done.4.a_ref = bf16[64,1024]{1,0:T(8,128)(2,1)S(1)} collective-permute-done((bf16[64,1024]{1,0:T(8,128)(2,1)S(1)}, bf16[64,1024]{1,0:T(8,128)(2,1)S(1)}, u32[]{:S(2)}, u32[]{:S(2)}) %collective-permute-start.4) | collective-permute-done | bytes 131104 | tf_op jit(solution)/shard_map/ppermute | solution.py:435
  13.2 6.0 %collective-permute-done.5.b_ref = bf16[64,1024]{1,0:T(8,128)(2,1)S(1)} collective-permute-done((bf16[64,1024]{1,0:T(8,128)(2,1)S(1)}, bf16[64,1024]{1,0:T(8,128)(2,1)S(1)}, u32[]{:S(2)}, u32[]{:S(2)}) %collective-permute-start.5) | collective-permute-done | bytes 131104 | tf_op jit(solution)/shard_map/ppermute | solution.py:435
  19.2 0.1 stack_pair.3.refs_1_
  19.3 1.6 %collective-permute-start.9 = (bf16[8,128,128]{2,1,0:T(8,128)(2,1)S(1)}, bf16[8,128,128]{2,1,0:T(8,128)(2,1)S(1)}, u32[]{:S(2)}, u32[]{:S(2)}) collective-permute-start(bf16[8,128,128]{2,1,0:T(8,128)(2,1)S(1)} %stack_pair.3.refs_1_), channel_id=1, source_target_pairs={{0,8},{4,12},{8,0},{12,4},{16,24},{20,28},{24,16},{28,20},{1,9},{5... | collective-permute-start | bytes 786440 | tf_op jit(solution)/shard_map/ppermute | solution.py:435
  20.8 0.5 collective-permute-start.13
  21.4 1.5 %collective-permute-start.17 = (bf16[8,128,128]{2,1,0:T(8,128)(2,1)S(1)}, bf16[8,128,128]{2,1,0:T(8,128)(2,1)S(1)}, u32[]{:S(2)}, u32[]{:S(2)}) collective-permute-start(bf16[8,128,128]{2,1,0:T(8,128)(2,1)S(1)} %stack_pair.3.refs_1_), channel_id=1, source_target_pairs={{0,24},{4,28},{8,16},{12,20},{16,8},{20,12},{24,0},{28,4},{1,25},{... | collective-permute-start | bytes 786440 | tf_op jit(solution)/shard_map/ppermute | solution.py:435
  22.8 0.1 stack_pair.2.refs_0_
  22.9 0.0 collective-permute-done.refs_1_
  22.9 1.6 %collective-permute-start.8 = (bf16[8,128,128]{2,1,0:T(8,128)(2,1)S(1)}, bf16[8,128,128]{2,1,0:T(8,128)(2,1)S(1)}, u32[]{:S(2)}, u32[]{:S(2)}) collective-permute-start(bf16[8,128,128]{2,1,0:T(8,128)(2,1)S(1)} %stack_pair.2.refs_0_), channel_id=1, source_target_pairs={{0,8},{4,12},{8,0},{12,4},{16,24},{20,28},{24,16},{28,20},{1,9},{5... | collective-permute-start | bytes 786440 | tf_op jit(solution)/shard_map/ppermute | solution.py:435
  24.5 0.0 collective-permute-done.1.refs_2_
  24.5 2.1 %collective-permute-start.2 = (bf16[64,1024]{1,0:T(8,128)(2,1)S(1)}, bf16[64,1024]{1,0:T(8,128)(2,1)S(1)}, u32[]{:S(2)}, u32[]{:S(2)}) collective-permute-start(bf16[64,1024]{1,0:T(8,128)(2,1)S(1)} %get-tuple-element.23), channel_id=1, source_target_pairs={{0,3},{1,2},{2,1},{3,0},{4,7},{5,6},{6,5},{7,4},{8,11},{9,10},{10,... | collective-permute-start | bytes 393224 | tf_op jit(solution)/shard_map/ppermute | solution.py:435
  26.6 5.6 %collective-permute-done.2.refs_3_ = bf16[64,1024]{1,0:T(8,128)(2,1)S(1)} collective-permute-done((bf16[64,1024]{1,0:T(8,128)(2,1)S(1)}, bf16[64,1024]{1,0:T(8,128)(2,1)S(1)}, u32[]{:S(2)}, u32[]{:S(2)}) %collective-permute-start.2) | collective-permute-done | bytes 131104 | tf_op jit(solution)/shard_map/ppermute | solution.py:435
  32.2 0.5 collective-permute-start.12
  32.7 1.7 %collective-permute-start.16 = (bf16[8,128,128]{2,1,0:T(8,128)(2,1)S(1)}, bf16[8,128,128]{2,1,0:T(8,128)(2,1)S(1)}, u32[]{:S(2)}, u32[]{:S(2)}) collective-permute-start(bf16[8,128,128]{2,1,0:T(8,128)(2,1)S(1)} %stack_pair.2.refs_0_), channel_id=1, source_target_pairs={{0,24},{4,28},{8,16},{12,20},{16,8},{20,12},{24,0},{28,4},{1,25},{... | collective-permute-start | bytes 786440 | tf_op jit(solution)/shard_map/ppermute | solution.py:435
  34.4 0.9 %collective-permute-done.13.refs_9_ = bf16[8,128,128]{2,1,0:T(8,128)(2,1)S(1)} collective-permute-done((bf16[8,128,128]{2,1,0:T(8,128)(2,1)S(1)}, bf16[8,128,128]{2,1,0:T(8,128)(2,1)S(1)}, u32[]{:S(2)}, u32[]{:S(2)}) %collective-permute-start.13) | collective-permute-done | bytes 262176 | tf_op jit(solution)/shard_map/ppermute | solution.py:435
  35.3 0.0 collective-permute-start.7
  35.3 0.0 collective-permute-done.17.refs_13_
  35.3 0.5 collective-permute-start.6
  35.8 4.0 %collective-permute-done.8.refs_4_ = bf16[8,128,128]{2,1,0:T(8,128)(2,1)S(1)} collective-permute-done((bf16[8,128,128]{2,1,0:T(8,128)(2,1)S(1)}, bf16[8,128,128]{2,1,0:T(8,128)(2,1)S(1)}, u32[]{:S(2)}, u32[]{:S(2)}) %collective-permute-start.8) | collective-permute-done | bytes 262176 | tf_op jit(solution)/shard_map/ppermute | solution.py:435
  39.8 0.0 collective-permute-start.11
  39.8 2.2 %copy-done = bf16[4096,512]{1,0:T(8,128)(2,1)S(1)} copy-done((bf16[4096,512]{1,0:T(8,128)(2,1)S(1)}, bf16[4096,512]{1,0:T(8,128)(2,1)}, u32[]{:S(2)}) %copy-start) | copy-done | bytes 4194328
  42.0 1.5 %turn_prefix_values.1.refs_5_ = bf16[4,144,4096]{2,1,0:T(8,128)(2,1)S(1)} custom-call(bf16[4096,512]{1,0:T(8,128)(2,1)S(1)} %copy-done), custom_call_target="tpu_custom_call" | custom-call | bytes 8388608 | tf_op jit(solution)/shard_map/turn_prefix_values/pallas_call | solution.py:217
  44.2 1.2 %collective-permute-done.12.refs_8_ = bf16[8,128,128]{2,1,0:T(8,128)(2,1)S(1)} collective-permute-done((bf16[8,128,128]{2,1,0:T(8,128)(2,1)S(1)}, bf16[8,128,128]{2,1,0:T(8,128)(2,1)S(1)}, u32[]{:S(2)}, u32[]{:S(2)}) %collective-permute-start.12) | collective-permute-done | bytes 262176 | tf_op jit(solution)/shard_map/ppermute | solution.py:435
  45.4 0.5 collective-permute-start.19
  46.0 0.1 collective-permute-start.10
  46.0 0.4 collective-permute-start.14
  46.5 0.1 collective-permute-start.18
  46.5 11.0 %attend_prefix.1 = (bf16[4,512,128]{2,1,0:T(8,128)(2,1)S(1)}, f32[4,8,512]{2,1,0:T(8,128)S(1)}, f32[4,144,512]{2,1,0:T(8,128)S(1)}) custom-call(s32[1]{0:T(128)S(6)} %copy.7.start_ref, bf16[64,1024]{1,0:T(8,128)(2,1)S(1)} %get-tuple-element.20.refs_0_, bf16[64,1024]{1,0:T(8,128)(2,1)S(1)} %collective-permute-done.refs_1_, ...), custom_call_target="tpu_custom_call" | custom-call | flops 4294967296 | bytes 8388608 | tf_op jit(solution)/shard_map/attend_prefix/pallas_call | solution.py:334
  57.5 0.0 collective-permute-done.15.refs_11_
  57.6 0.0 collective-permute-done.10.refs_6_
  57.6 0.0 collective-permute-done.14.refs_10_
  57.6 8.0 %attend_span.1 = (bf16[64,1024]{1,0:T(8,128)(2,1)S(1)}, bf16[64,1024]{1,0:T(8,128)(2,1)S(1)}, bf16[64,1024]{1,0:T(8,128)(2,1)S(1)}, bf16[64,1024]{1,0:T(8,128)(2,1)S(1)}) custom-call(bf16[4,512,128]{2,1,0:T(8,128)(2,1)S(1)} %get-tuple-element.24.q_ref, f32[4,8,512]{2,1,0:T(8,128)S(1)} %get-tuple-element.25.m_in, ...), custom_call_target="tpu_custom_call" | custom-call | flops 2147483648 | bytes 4194304 | tf_op jit(solution)/shard_map/attend_span/pallas_call | solution.py:414
  65.6 0.1 collective-permute-start.20
  65.7 1.6 %collective-permute-start.21 = (bf16[64,1024]{1,0:T(8,128)(2,1)S(1)}, bf16[64,1024]{1,0:T(8,128)(2,1)S(1)}, u32[]{:S(2)}, u32[]{:S(2)}) collective-permute-start(bf16[64,1024]{1,0:T(8,128)(2,1)S(1)} %get-tuple-element.33), channel_id=1, source_target_pairs={{0,2},{1,3},{2,0},{3,1},{4,6},{5,7},{6,4},{7,5},{8,10},{9,11},{10,... | collective-permute-start | bytes 393224 | tf_op jit(solution)/shard_map/ppermute | solution.py:435
  67.3 1.8 %collective-permute-start.22 = (bf16[64,1024]{1,0:T(8,128)(2,1)S(1)}, bf16[64,1024]{1,0:T(8,128)(2,1)S(1)}, u32[]{:S(2)}, u32[]{:S(2)}) collective-permute-start(bf16[64,1024]{1,0:T(8,128)(2,1)S(1)} %get-tuple-element.34), channel_id=1, source_target_pairs={{0,3},{1,2},{2,1},{3,0},{4,7},{5,6},{6,5},{7,4},{8,11},{9,10},{10,... | collective-permute-start | bytes 393224 | tf_op jit(solution)/shard_map/ppermute | solution.py:435
  69.1 2.8 %collective-permute-done.20.refs_1_ = bf16[64,1024]{1,0:T(8,128)(2,1)S(1)} collective-permute-done((bf16[64,1024]{1,0:T(8,128)(2,1)S(1)}, bf16[64,1024]{1,0:T(8,128)(2,1)S(1)}, u32[]{:S(2)}, u32[]{:S(2)}) %collective-permute-start.20) | collective-permute-done | bytes 131104 | tf_op jit(solution)/shard_map/ppermute | solution.py:435
  72.0 4.7 %collective-permute-done.21.refs_2_ = bf16[64,1024]{1,0:T(8,128)(2,1)S(1)} collective-permute-done((bf16[64,1024]{1,0:T(8,128)(2,1)S(1)}, bf16[64,1024]{1,0:T(8,128)(2,1)S(1)}, u32[]{:S(2)}, u32[]{:S(2)}) %collective-permute-start.21) | collective-permute-done | bytes 131104 | tf_op jit(solution)/shard_map/ppermute | solution.py:435
  76.7 4.4 %collective-permute-done.22.refs_3_ = bf16[64,1024]{1,0:T(8,128)(2,1)S(1)} collective-permute-done((bf16[64,1024]{1,0:T(8,128)(2,1)S(1)}, bf16[64,1024]{1,0:T(8,128)(2,1)S(1)}, u32[]{:S(2)}, u32[]{:S(2)}) %collective-permute-start.22) | collective-permute-done | bytes 131104 | tf_op jit(solution)/shard_map/ppermute | solution.py:435
  81.1 0.8 join_planes.1
  (15 shorter events, 0.0 us)
Async XLA Ops:
  0.0 1.0 %copy-start.1 = (bf16[64,4096]{1,0:T(8,128)(2,1)S(1)}, bf16[64,4096]{1,0:T(8,128)(2,1)}, u32[]{:S(2)}) copy-start(bf16[64,4096]{1,0:T(8,128)(2,1)} %q_ref.1) | copy-start | bytes 1572868
  1.0 0.9 %copy-start.2 = (bf16[64,2048]{1,0:T(8,128)(2,1)S(1)}, bf16[64,2048]{1,0:T(8,128)(2,1)}, u32[]{:S(2)}) copy-start(bf16[64,2048]{1,0:T(8,128)(2,1)} %k_ref.1) | copy-start | bytes 786436
  2.0 0.9 %copy-start.3 = (bf16[64,2048]{1,0:T(8,128)(2,1)S(1)}, bf16[64,2048]{1,0:T(8,128)(2,1)}, u32[]{:S(2)}) copy-start(bf16[64,2048]{1,0:T(8,128)(2,1)} %v_ref.2) | copy-start | bytes 786436
  3.3 9.9 %collective-permute-start.4 = (bf16[64,1024]{1,0:T(8,128)(2,1)S(1)}, bf16[64,1024]{1,0:T(8,128)(2,1)S(1)}, u32[]{:S(2)}, u32[]{:S(2)}) collective-permute-start(bf16[64,1024]{1,0:T(8,128)(2,1)S(1)} %get-tuple-element.29), channel_id=1, source_target_pairs={{0,2},{1,3},{2,0},{3,1},{4,6},{5,7},{6,4},{7,5},{8,10},{9,11},{10,... | collective-permute-start | bytes 393224 | tf_op jit(solution)/shard_map/ppermute | solution.py:435
  3.7 15.5 %collective-permute-start.5 = (bf16[64,1024]{1,0:T(8,128)(2,1)S(1)}, bf16[64,1024]{1,0:T(8,128)(2,1)S(1)}, u32[]{:S(2)}, u32[]{:S(2)}) collective-permute-start(bf16[64,1024]{1,0:T(8,128)(2,1)S(1)} %get-tuple-element.30), channel_id=1, source_target_pairs={{0,3},{1,2},{2,1},{3,0},{4,7},{5,6},{6,5},{7,4},{8,11},{9,10},{10,... | collective-permute-start | bytes 393224 | tf_op jit(solution)/shard_map/ppermute | solution.py:435
  6.4 15.0 %collective-permute-start.3 = (bf16[64,1024]{1,0:T(8,128)(2,1)S(1)}, bf16[64,1024]{1,0:T(8,128)(2,1)S(1)}, u32[]{:S(2)}, u32[]{:S(2)}) collective-permute-start(bf16[64,1024]{1,0:T(8,128)(2,1)S(1)} %get-tuple-element.28), channel_id=1, source_target_pairs={{0,1},{1,0},{2,3},{3,2},{4,5},{5,4},{6,7},{7,6},{8,9},{9,8},{10,11... | collective-permute-start | bytes 393224 | tf_op jit(solution)/shard_map/ppermute | solution.py:435
  7.7 15.2 %collective-permute-start = (bf16[64,1024]{1,0:T(8,128)(2,1)S(1)}, bf16[64,1024]{1,0:T(8,128)(2,1)S(1)}, u32[]{:S(2)}, u32[]{:S(2)}) collective-permute-start(bf16[64,1024]{1,0:T(8,128)(2,1)S(1)} %get-tuple-element.21), channel_id=1, source_target_pairs={{0,1},{1,0},{2,3},{3,2},{4,5},{5,4},{6,7},{7,6},{8,9},{9,8},{10,11... | collective-permute-start | bytes 393224 | tf_op jit(solution)/shard_map/ppermute | solution.py:435
  8.4 16.1 %collective-permute-start.1 = (bf16[64,1024]{1,0:T(8,128)(2,1)S(1)}, bf16[64,1024]{1,0:T(8,128)(2,1)S(1)}, u32[]{:S(2)}, u32[]{:S(2)}) collective-permute-start(bf16[64,1024]{1,0:T(8,128)(2,1)S(1)} %get-tuple-element.22), channel_id=1, source_target_pairs={{0,2},{1,3},{2,0},{3,1},{4,6},{5,7},{6,4},{7,5},{8,10},{9,11},{10,... | collective-permute-start | bytes 393224 | tf_op jit(solution)/shard_map/ppermute | solution.py:435
  19.3 13.4 %collective-permute-start.9 = (bf16[8,128,128]{2,1,0:T(8,128)(2,1)S(1)}, bf16[8,128,128]{2,1,0:T(8,128)(2,1)S(1)}, u32[]{:S(2)}, u32[]{:S(2)}) collective-permute-start(bf16[8,128,128]{2,1,0:T(8,128)(2,1)S(1)} %stack_pair.3.refs_1_), channel_id=1, source_target_pairs={{0,8},{4,12},{8,0},{12,4},{16,24},{20,28},{24,16},{28,20},{1,9},{5... | collective-permute-start | bytes 786440 | tf_op jit(solution)/shard_map/ppermute | solution.py:435
  20.8 14.5 %collective-permute-start.13 = (bf16[8,128,128]{2,1,0:T(8,128)(2,1)S(1)}, bf16[8,128,128]{2,1,0:T(8,128)(2,1)S(1)}, u32[]{:S(2)}, u32[]{:S(2)}) collective-permute-start(bf16[8,128,128]{2,1,0:T(8,128)(2,1)S(1)} %stack_pair.3.refs_1_), channel_id=1, source_target_pairs={{0,16},{4,20},{8,24},{12,28},{16,0},{20,4},{24,8},{28,12},{1,17},{... | collective-permute-start | bytes 786440 | tf_op jit(solution)/shard_map/ppermute | solution.py:435
  21.4 14.0 %collective-permute-start.17 = (bf16[8,128,128]{2,1,0:T(8,128)(2,1)S(1)}, bf16[8,128,128]{2,1,0:T(8,128)(2,1)S(1)}, u32[]{:S(2)}, u32[]{:S(2)}) collective-permute-start(bf16[8,128,128]{2,1,0:T(8,128)(2,1)S(1)} %stack_pair.3.refs_1_), channel_id=1, source_target_pairs={{0,24},{4,28},{8,16},{12,20},{16,8},{20,12},{24,0},{28,4},{1,25},{... | collective-permute-start | bytes 786440 | tf_op jit(solution)/shard_map/ppermute | solution.py:435
  22.9 16.9 %collective-permute-start.8 = (bf16[8,128,128]{2,1,0:T(8,128)(2,1)S(1)}, bf16[8,128,128]{2,1,0:T(8,128)(2,1)S(1)}, u32[]{:S(2)}, u32[]{:S(2)}) collective-permute-start(bf16[8,128,128]{2,1,0:T(8,128)(2,1)S(1)} %stack_pair.2.refs_0_), channel_id=1, source_target_pairs={{0,8},{4,12},{8,0},{12,4},{16,24},{20,28},{24,16},{28,20},{1,9},{5... | collective-permute-start | bytes 786440 | tf_op jit(solution)/shard_map/ppermute | solution.py:435
  24.5 7.7 %collective-permute-start.2 = (bf16[64,1024]{1,0:T(8,128)(2,1)S(1)}, bf16[64,1024]{1,0:T(8,128)(2,1)S(1)}, u32[]{:S(2)}, u32[]{:S(2)}) collective-permute-start(bf16[64,1024]{1,0:T(8,128)(2,1)S(1)} %get-tuple-element.23), channel_id=1, source_target_pairs={{0,3},{1,2},{2,1},{3,0},{4,7},{5,6},{6,5},{7,4},{8,11},{9,10},{10,... | collective-permute-start | bytes 393224 | tf_op jit(solution)/shard_map/ppermute | solution.py:435
  32.2 13.3 %collective-permute-start.12 = (bf16[8,128,128]{2,1,0:T(8,128)(2,1)S(1)}, bf16[8,128,128]{2,1,0:T(8,128)(2,1)S(1)}, u32[]{:S(2)}, u32[]{:S(2)}) collective-permute-start(bf16[8,128,128]{2,1,0:T(8,128)(2,1)S(1)} %stack_pair.2.refs_0_), channel_id=1, source_target_pairs={{0,16},{4,20},{8,24},{12,28},{16,0},{20,4},{24,8},{28,12},{1,17},{... | collective-permute-start | bytes 786440 | tf_op jit(solution)/shard_map/ppermute | solution.py:435
  32.7 12.8 %collective-permute-start.16 = (bf16[8,128,128]{2,1,0:T(8,128)(2,1)S(1)}, bf16[8,128,128]{2,1,0:T(8,128)(2,1)S(1)}, u32[]{:S(2)}, u32[]{:S(2)}) collective-permute-start(bf16[8,128,128]{2,1,0:T(8,128)(2,1)S(1)} %stack_pair.2.refs_0_), channel_id=1, source_target_pairs={{0,24},{4,28},{8,16},{12,20},{16,8},{20,12},{24,0},{28,4},{1,25},{... | collective-permute-start | bytes 786440 | tf_op jit(solution)/shard_map/ppermute | solution.py:435
  35.3 10.7 %collective-permute-start.7 = (bf16[8,128,128]{2,1,0:T(8,128)(2,1)S(1)}, bf16[8,128,128]{2,1,0:T(8,128)(2,1)S(1)}, u32[]{:S(2)}, u32[]{:S(2)}) collective-permute-start(bf16[8,128,128]{2,1,0:T(8,128)(2,1)S(1)} %stack_pair.3.refs_1_), channel_id=1, source_target_pairs={{0,4},{4,0},{8,12},{12,8},{16,20},{20,16},{24,28},{28,24},{1,5},{5... | collective-permute-start | bytes 786440 | tf_op jit(solution)/shard_map/ppermute | solution.py:435
  35.3 10.7 %collective-permute-start.6 = (bf16[8,128,128]{2,1,0:T(8,128)(2,1)S(1)}, bf16[8,128,128]{2,1,0:T(8,128)(2,1)S(1)}, u32[]{:S(2)}, u32[]{:S(2)}) collective-permute-start(bf16[8,128,128]{2,1,0:T(8,128)(2,1)S(1)} %stack_pair.2.refs_0_), channel_id=1, source_target_pairs={{0,4},{4,0},{8,12},{12,8},{16,20},{20,16},{24,28},{28,24},{1,5},{5... | collective-permute-start | bytes 786440 | tf_op jit(solution)/shard_map/ppermute | solution.py:435
  39.8 6.6 %collective-permute-start.11 = (bf16[8,128,128]{2,1,0:T(8,128)(2,1)S(1)}, bf16[8,128,128]{2,1,0:T(8,128)(2,1)S(1)}, u32[]{:S(2)}, u32[]{:S(2)}) collective-permute-start(bf16[8,128,128]{2,1,0:T(8,128)(2,1)S(1)} %collective-permute-done.9.refs_5_), channel_id=1, source_target_pairs={{0,4},{4,0},{8,12},{12,8},{16,20},{20,16},{24,28},{28,24},{1,5},{5... | collective-permute-start | bytes 786440 | tf_op jit(solution)/shard_map/ppermute | solution.py:435
  39.8 2.2 %copy-start = (bf16[4096,512]{1,0:T(8,128)(2,1)S(1)}, bf16[4096,512]{1,0:T(8,128)(2,1)}, u32[]{:S(2)}) copy-start(bf16[4096,512]{1,0:T(8,128)(2,1)} %v_ref.3) | copy-start | bytes 12582916
  42.0 4.5 %copy-start.4 = (bf16[4096,512]{1,0:T(8,128)(2,1)S(1)}, bf16[4096,512]{1,0:T(8,128)(2,1)}, u32[]{:S(2)}) copy-start(bf16[4096,512]{1,0:T(8,128)(2,1)} %refs_4_.1) | copy-start | bytes 12582916
  45.4 12.1 %collective-permute-start.15 = (bf16[8,128,128]{2,1,0:T(8,128)(2,1)S(1)}, bf16[8,128,128]{2,1,0:T(8,128)(2,1)S(1)}, u32[]{:S(2)}, u32[]{:S(2)}) collective-permute-start(bf16[8,128,128]{2,1,0:T(8,128)(2,1)S(1)} %collective-permute-done.13.refs_9_), channel_id=1, source_target_pairs={{0,4},{4,0},{8,12},{12,8},{16,20},{20,16},{24,28},{28,24},{1,5},{5... | collective-permute-start | bytes 786440 | tf_op jit(solution)/shard_map/ppermute | solution.py:435
  45.4 12.1 %collective-permute-start.19 = (bf16[8,128,128]{2,1,0:T(8,128)(2,1)S(1)}, bf16[8,128,128]{2,1,0:T(8,128)(2,1)S(1)}, u32[]{:S(2)}, u32[]{:S(2)}) collective-permute-start(bf16[8,128,128]{2,1,0:T(8,128)(2,1)S(1)} %collective-permute-done.17.refs_13_), channel_id=1, source_target_pairs={{0,4},{4,0},{8,12},{12,8},{16,20},{20,16},{24,28},{28,24},{1,5},{5... | collective-permute-start | bytes 786440 | tf_op jit(solution)/shard_map/ppermute | solution.py:435
  46.0 11.6 %collective-permute-start.10 = (bf16[8,128,128]{2,1,0:T(8,128)(2,1)S(1)}, bf16[8,128,128]{2,1,0:T(8,128)(2,1)S(1)}, u32[]{:S(2)}, u32[]{:S(2)}) collective-permute-start(bf16[8,128,128]{2,1,0:T(8,128)(2,1)S(1)} %collective-permute-done.8.refs_4_), channel_id=1, source_target_pairs={{0,4},{4,0},{8,12},{12,8},{16,20},{20,16},{24,28},{28,24},{1,5},{5... | collective-permute-start | bytes 786440 | tf_op jit(solution)/shard_map/ppermute | solution.py:435
  46.0 11.6 %collective-permute-start.14 = (bf16[8,128,128]{2,1,0:T(8,128)(2,1)S(1)}, bf16[8,128,128]{2,1,0:T(8,128)(2,1)S(1)}, u32[]{:S(2)}, u32[]{:S(2)}) collective-permute-start(bf16[8,128,128]{2,1,0:T(8,128)(2,1)S(1)} %collective-permute-done.12.refs_8_), channel_id=1, source_target_pairs={{0,4},{4,0},{8,12},{12,8},{16,20},{20,16},{24,28},{28,24},{1,5},{5... | collective-permute-start | bytes 786440 | tf_op jit(solution)/shard_map/ppermute | solution.py:435
  46.5 11.1 %collective-permute-start.18 = (bf16[8,128,128]{2,1,0:T(8,128)(2,1)S(1)}, bf16[8,128,128]{2,1,0:T(8,128)(2,1)S(1)}, u32[]{:S(2)}, u32[]{:S(2)}) collective-permute-start(bf16[8,128,128]{2,1,0:T(8,128)(2,1)S(1)} %collective-permute-done.16.refs_12_), channel_id=1, source_target_pairs={{0,4},{4,0},{8,12},{12,8},{16,20},{20,16},{24,28},{28,24},{1,5},{5... | collective-permute-start | bytes 786440 | tf_op jit(solution)/shard_map/ppermute | solution.py:435
  65.6 6.4 %collective-permute-start.20 = (bf16[64,1024]{1,0:T(8,128)(2,1)S(1)}, bf16[64,1024]{1,0:T(8,128)(2,1)S(1)}, u32[]{:S(2)}, u32[]{:S(2)}) collective-permute-start(bf16[64,1024]{1,0:T(8,128)(2,1)S(1)} %get-tuple-element.32), channel_id=1, source_target_pairs={{0,1},{1,0},{2,3},{3,2},{4,5},{5,4},{6,7},{7,6},{8,9},{9,8},{10,11... | collective-permute-start | bytes 393224 | tf_op jit(solution)/shard_map/ppermute | solution.py:435
  65.7 11.0 %collective-permute-start.21 = (bf16[64,1024]{1,0:T(8,128)(2,1)S(1)}, bf16[64,1024]{1,0:T(8,128)(2,1)S(1)}, u32[]{:S(2)}, u32[]{:S(2)}) collective-permute-start(bf16[64,1024]{1,0:T(8,128)(2,1)S(1)} %get-tuple-element.33), channel_id=1, source_target_pairs={{0,2},{1,3},{2,0},{3,1},{4,6},{5,7},{6,4},{7,5},{8,10},{9,11},{10,... | collective-permute-start | bytes 393224 | tf_op jit(solution)/shard_map/ppermute | solution.py:435
  67.3 13.8 %collective-permute-start.22 = (bf16[64,1024]{1,0:T(8,128)(2,1)S(1)}, bf16[64,1024]{1,0:T(8,128)(2,1)S(1)}, u32[]{:S(2)}, u32[]{:S(2)}) collective-permute-start(bf16[64,1024]{1,0:T(8,128)(2,1)S(1)} %get-tuple-element.34), channel_id=1, source_target_pairs={{0,3},{1,2},{2,1},{3,0},{4,7},{5,6},{6,5},{7,4},{8,11},{9,10},{10,... | collective-permute-start | bytes 393224 | tf_op jit(solution)/shard_map/ppermute | solution.py:435
